TPU v7x, 32 devices: a whole 2x2x4 slice. The times are simulated.
32 devices in a mesh: gx: 8 (over y, x, core), gy: 4 (over z).
Axes of the slice: x: 2, y: 2, z: 4, core: 2. Of those that a mesh axis runs over, the one named last changes fastest.
Arguments:
- cotangent: float32 [3, 16, 8, 128], P(None, 'gx', 'gy'), may hold values from -4 to 4
- polarizability: float32 [16, 8, 128], P('gx', 'gy'), may hold values from 0.2 to 1.6
- site_offset: int32 [3, 16, 8, 128], P(None, 'gx', 'gy'), may hold values from 0 to 15, as said below
- site_fraction: float32 [3, 16, 8, 128], P(None, 'gx', 'gy'), may hold values from 0.2 to 0.8
- cell_count: int32 [16, 8, 16], P('gx', 'gy'), may hold values from 4 to 8, as said below
Outputs:
- adjoint_dipoles: float32 [3, 16, 8, 128], P(None, 'gx', 'gy')
Inputs may be any that keep to these rules, and one draw needn't show every extreme that they name: `site_offset`: within a cell the 8 slots name distinct mesh points: no two slots have the same three components. The first component is below 8, the second below 8, the third below 16. `cell_count`: some cell holds 8 live atoms.
All inputs are finite; a program needn't handle non-finite values.
Results may differ from a plain program's by a relative error of at most 0.0001.
Values sent between devices are 32-bit elements; how exact they have to be, the bound alone decides.
No kernel may reach another device: no remote copies, remote signals or barrier semaphores. Data moves between devices by JAX's collectives and lax.ppermute only.
A program may use at most 128 MiB of HBM per device.

v0:
```python
import functools
import math

import jax
import jax.numpy as jnp
import ml_dtypes
import numpy as np
from jax import lax
from jax.experimental import pallas as pl
from jax.experimental.pallas import tpu as pltpu
from jax.sharding import PartitionSpec as P

A = 8
HX = 8
HY = 8
HZ = 16
ITERS = 2
BETA = 0.7
THOLE = 0.39
ROOT_PI = 1.7724538509055159
SELF_GAIN = 4.0 * BETA * BETA * BETA / (3.0 * ROOT_PI)
MODES = 8
SPAN = 16
AXES = ("gx", "gy")
F32 = jnp.float32
BF16 = jnp.bfloat16
VMEM_LIMIT = 56 * 1024 * 1024


def two_terms(table):
    high = table.astype(ml_dtypes.bfloat16)
    low = (table - high.astype(np.float64)).astype(ml_dtypes.bfloat16)
    return high, low


def cas_table(length):
    grid = np.arange(length, dtype=np.int64)
    angle = 2.0 * np.pi / length * (grid[:, None] * grid[None, :] % length)
    return np.cos(angle) + np.sin(angle)


def x_tables(cells, length):
    cas = cas_table(length)
    place = (np.arange(cells)[:, None] * HX + np.arange(SPAN)[None, :]) % length
    forward = np.broadcast_to(cas[place][:, None], (cells, 2, SPAN, length))
    forward = forward.reshape(cells // 4, 4 * 2 * SPAN, length)
    inverse = np.broadcast_to(cas[place][:, None], (cells, 4, SPAN, length))
    inverse = inverse.reshape(cells // 2, 2 * 4 * SPAN, length).transpose(0, 2, 1)
    return two_terms(forward), two_terms(inverse)


def split(value):
    high = value.astype(BF16)
    low = (value - high.astype(F32)).astype(BF16)
    return high, low


def dot(left, right):
    return jnp.dot(left, right, preferred_element_type=F32)


def dot_nt(left, right):
    return lax.dot_general(left, right, (((1,), (1,)), ((), ())), preferred_element_type=F32)


def spline(fraction):
    rest = 1.0 - fraction
    square = fraction * fraction
    cube = square * fraction
    values = (
        rest * rest * rest / 6.0,
        (3.0 * cube - 6.0 * square + 4.0) / 6.0,
        (-3.0 * cube + 3.0 * square + 3.0 * fraction + 1.0) / 6.0,
        cube / 6.0,
    )
    slopes = (
        -0.5 * rest * rest,
        0.5 * (3.0 * square - 4.0 * fraction),
        0.5 * (-3.0 * square + 2.0 * fraction + 1.0),
        0.5 * square,
    )
    return values, slopes


def basis(anchor, weights):
    lanes = anchor.shape[1]
    index = lax.broadcasted_iota(jnp.int32, (SPAN, lanes), 0) - anchor
    total = jnp.zeros((SPAN, lanes), F32)
    for order in range(4):
        total = jnp.where(index == order, weights[order], total)
    return total


def turns(count, length):
    part = count.astype(F32) * (1.0 / length)
    half = math.pi * jnp.where(2 * count >= length, part - 1.0, part)
    square = half * half
    sine = 1.0
    for order in (10, 8, 6, 4, 2):
        sine = 1.0 - square * sine * (1.0 / (order * (order + 1)))
    sine = sine * half
    cosine = 1.0
    for order in (11, 9, 7, 5, 3, 1):
        cosine = 1.0 - square * cosine * (1.0 / (order * (order + 1)))
    return 1.0 - 2.0 * sine * sine, 2.0 * sine * cosine


def pack_kernel(cot_ref, polar_ref, offset_ref, fraction_ref, count_ref, send_ref, gain_ref):
    cells_x, cells_y, lanes = polar_ref.shape
    devices = send_ref.shape[0]
    cells = lanes // A
    row = lax.broadcasted_iota(jnp.int32, (cells, lanes), 0)
    lane = lax.broadcasted_iota(jnp.int32, (cells, lanes), 1)
    widen = jnp.where(lane // A == row, 1.0, 0.0)
    slot = (lax.broadcasted_iota(jnp.int32, (cells_y, lanes), 1) % A).astype(F32)
    rows = [[] for _ in range(7)]
    gains = []
    for cx in range(cells_x):
        count = dot(count_ref[cx].astype(F32), widen)
        gain = jnp.where(slot < count, polar_ref[cx], 0.0)
        gains.append(gain)
        for axis in range(3):
            place = offset_ref[axis, cx].astype(F32) + 1.0 + fraction_ref[axis, cx]
            rows[axis].append(place)
            rows[3 + axis].append(gain * cot_ref[axis, cx])
        rows[6].append(polar_ref[cx])
    gain_ref[...] = jnp.concatenate(gains, axis=0)
    block = jnp.stack([jnp.concatenate(parts, axis=0) for parts in rows], axis=0)

    def put(d, carry):
        send_ref[d] = block
        return carry

    lax.fori_loop(0, devices, put, 0)


def far_kernel(
    shape,
    place_ref,
    moment_ref,
    mode_ref,
    phase_ref,
    green_ref,
    fx_high_ref,
    fx_low_ref,
    ix_high_ref,
    ix_low_ref,
    y_ref,
    out_ref,
    cell_ref,
    line_ref,
    back_ref,
    wave_ref,
    side_ref,
    rise_ref,
    edge_ref,
):
    devices_x, devices_y, cells_x, cells_y, points_z = shape
    columns = cells_x * cells_y
    lanes = place_ref.shape[3]
    length_x = green_ref.shape[1]
    length_y = y_ref.shape[0]
    tall = length_y * MODES
    spill = 3 * MODES
    reach = (HY + 3) * MODES
    per_cell = HY * MODES
    turn_x = 4 // cells_x
    keep = side_ref.shape[0] > 1
    layer = (lax.broadcasted_iota(jnp.int32, (1, lanes), 1) // A) * HZ
    cell_ref[...] = jnp.zeros_like(cell_ref)

    def statics(d, l):
        k = d if keep else 0
        place = [place_ref[d, axis, l : l + 1, :] for axis in range(3)]
        whole = [jnp.floor(value) for value in place]
        parts = [spline(value - low) for value, low in zip(place, whole)]
        anchor = [low.astype(jnp.int32) - 1 for low in whole]
        values_x = basis(anchor[0], parts[0][0])
        slopes_x = basis(anchor[0], parts[0][1])
        side = jnp.concatenate([slopes_x, values_x], axis=1)
        high, low = split(side)
        side_ref[k, l] = jnp.concatenate([high, low], axis=0)
        rise_ref[k, l] = jnp.concatenate(
            [basis(anchor[1], parts[1][0]), basis(anchor[1], parts[1][1])], axis=0
        )
        phase = lax.rem(mode_ref[...] * (anchor[2] + layer), points_z)
        cosine, sine = turns(phase, points_z)
        found = []
        for weights in parts[2]:
            plus = weights[0] * phase_ref[0]
            minus = weights[0] * phase_ref[4]
            for order in range(1, 4):
                plus = plus + weights[order] * phase_ref[order]
                minus = minus + weights[order] * phase_ref[4 + order]
            found.append(cosine * plus + sine * minus)
        edge_ref[k, l] = jnp.concatenate(found, axis=0)

    def spread(d, l, slot, group, start):
        k = d if keep else 0
        first = edge_ref[k, l, :MODES] * moment_ref[d, 0, l : l + 1, :]
        second = edge_ref[k, l, :MODES] * moment_ref[d, 1, l : l + 1, :]
        third = edge_ref[k, l, MODES:] * moment_ref[d, 2, l : l + 1, :]
        tiles = []
        for y in range(HY + 3):
            value = rise_ref[k, l, y : y + 1, :]
            slope = rise_ref[k, l, SPAN + y : SPAN + y + 1, :]
            tile = jnp.concatenate([value * first, slope * second + value * third], axis=1)
            rest = tile - tile.astype(BF16).astype(F32)
            tiles.append(jnp.concatenate([tile, rest], axis=0).astype(BF16))
        sums = jnp.concatenate(tiles, axis=0)
        pieces = []
        if slot:
            pieces.append(jnp.zeros((slot * 2 * SPAN, 2 * lanes), BF16))
        pieces.append(side_ref[k, l])
        if slot < 3:
            pieces.append(jnp.zeros(((3 - slot) * 2 * SPAN, 2 * lanes), BF16))
        got = dot_nt(sums, jnp.concatenate(pieces, axis=0))
        got = got.reshape(HY + 3, 2, MODES, got.shape[1])
        got = (got[:, 0] + got[:, 1]).reshape(reach, got.shape[3])
        cell_ref[group, pl.ds(start, reach), :] = cell_ref[group, pl.ds(start, reach), :] + got

    def spread_row(pair, carry):
        for odd in range(turn_x):
            gx = pair * turn_x + odd

            def spread_device(gy, inner):
                d = gx * devices_y + gy
                for l in range(columns):
                    statics(d, l)
                for l in range(columns):
                    slot = odd * cells_x + l // cells_y
                    start = pl.multiple_of(
                        (gy * cells_y + l % cells_y) * per_cell, per_cell
                    )
                    spread(d, l, slot, pair, start)
                return inner

            lax.fori_loop(0, devices_y, spread_device, 0)
        return carry

    lax.fori_loop(0, devices_x // turn_x, spread_row, 0)

    cell_ref[:, :spill, :] = cell_ref[:, :spill, :] + cell_ref[:, tall : tall + spill, :]
    total = jnp.zeros((tall, length_x), F32)
    for group in range(cell_ref.shape[0]):
        high, low = split(cell_ref[group, :tall, :])
        total = total + (
            dot(high, fx_high_ref[group])
            + dot(low, fx_high_ref[group])
            + dot(high, fx_low_ref[group])
        )
    blocks = length_x // line_ref.shape[2]
    width = line_ref.shape[2]
    for block in range(blocks):
        line_ref[block] = total[:, block * width : (block + 1) * width]

    def along_y(value):
        high, low = split(value)
        return dot(y_ref[...], jnp.concatenate([high, high, low], axis=0))

    for mode in range(MODES):
        for block in range(blocks):
            got = along_y(line_ref[block, pl.ds(mode, length_y, stride=MODES), :])
            got = got * green_ref[
                mode * length_y : (mode + 1) * length_y, block * width : (block + 1) * width
            ]
            back_ref[block, pl.ds(mode, length_y, stride=MODES), :] = along_y(got)
    high, low = split(jnp.concatenate([back_ref[block] for block in range(blocks)], axis=1))
    lane = lax.broadcasted_iota(jnp.int32, (tall, 2 * 4 * SPAN), 1)
    rest = lane // SPAN % 2 == 1
    for group in range(wave_ref.shape[0]):
        got = (
            dot(high, ix_high_ref[group])
            + dot(low, ix_high_ref[group])
            + dot(high, ix_low_ref[group])
        )
        got = jnp.where(rest, got - got.astype(BF16).astype(F32), got).astype(BF16)
        wave_ref[group, :tall, :] = got
        wave_ref[group, tall:, :] = got[: wave_ref.shape[1] - tall]

    window = -(-reach // 16) * 16

    def gather(d, l, slot, group, start):
        k = d if keep else 0
        high = side_ref[k, l, :SPAN]
        low = side_ref[k, l, SPAN:]
        block = [high, high, low, low]
        zero = jnp.zeros((4 * SPAN, 2 * lanes), BF16)
        pieces = [zero] + block if slot else block + [zero]
        got = dot(wave_ref[group, pl.ds(start, window), :], jnp.concatenate(pieces, axis=0))
        sums = [jnp.zeros((MODES, lanes), F32) for _ in range(3)]
        for y in range(HY + 3):
            value = rise_ref[k, l, y : y + 1, :]
            slope = rise_ref[k, l, SPAN + y : SPAN + y + 1, :]
            sloped = got[y * MODES : (y + 1) * MODES, :lanes]
            plain = got[y * MODES : (y + 1) * MODES, lanes:]
            sums[0] = sums[0] + sloped * value
            sums[1] = sums[1] + plain * slope
            sums[2] = sums[2] + plain * value
        value = edge_ref[k, l, :MODES]
        slope = edge_ref[k, l, MODES:]
        for axis, part in enumerate((value, value, slope)):
            out_ref[d, axis, l : l + 1, :] = -jnp.sum(sums[axis] * part, axis=0, keepdims=True)

    def gather_row(gx, carry):
        def gather_device(gy, inner):
            d = gx * devices_y + gy
            if not keep:
                for l in range(columns):
                    statics(d, l)
            for l in range(columns):
                across = l // cells_y
                start = pl.multiple_of((gy * cells_y + l % cells_y) * per_cell, per_cell)
                group = (gx * cells_x + across - across % 2) // 2
                gather(d, l, across % 2, group, start)
            return inner

        lax.fori_loop(0, devices_y, gather_device, 0)
        return carry

    lax.fori_loop(0, devices_x, gather_row, 0)


def near_kernel(shape, where_ref, static_ref, moment_ref, out_ref, raw_ref, wide_ref, sum_ref):
    devices_x, devices_y, cells_x, cells_y = shape
    lanes = static_ref.shape[3]
    rows_x, rows_y = cells_x + 2, cells_y + 2
    total_x, total_y = devices_x * cells_x, devices_y * cells_y
    lane = lax.broadcasted_iota(jnp.int32, (A, lanes), 1)
    sub = lax.broadcasted_iota(jnp.int32, (A, lanes), 0)
    own = lane % A == sub
    for a in range(rows_x):
        for b in range(rows_y):
            cell_x = lax.rem(where_ref[0] * cells_x + (a - 1 + total_x), total_x)
            cell_y = lax.rem(where_ref[1] * cells_y + (b - 1 + total_y), total_y)
            d = (cell_x // cells_x) * devices_y + cell_y // cells_y
            l = lax.rem(cell_x, cells_x) * cells_y + lax.rem(cell_y, cells_y)
            for item in range(7):
                if item < 4:
                    row = static_ref[d, item if item < 3 else 6, pl.ds(l, 1), :]
                else:
                    row = moment_ref[d, item - 4, pl.ds(l, 1), :]
                first = ((a * rows_y + b) * 7 + item) * A
                raw_ref[first : first + A, :] = jnp.where(own, row, 0.0)
    group = lax.broadcasted_iota(jnp.int32, (lanes, lanes), 0) // A
    other = lax.broadcasted_iota(jnp.int32, (lanes, lanes), 1) // A
    ones = jnp.where(group == other, 1.0, 0.0).astype(BF16)
    raw = raw_ref[...]
    high = raw.astype(BF16)
    raw = raw - high.astype(F32)
    middle = raw.astype(BF16)
    low = (raw - middle.astype(F32)).astype(BF16)
    wide = dot(low, ones) + dot(middle, ones) + dot(high, ones)
    wide_ref[...] = wide.reshape(wide_ref.shape)

    for across in range(cells_x):
        for along in range(cells_y):
            mine = (across + 1) * rows_y + along + 1
            mine_d = where_ref[0] * devices_y + where_ref[1]
            mine_l = across * cells_y + along
            at = [static_ref[mine_d, axis, mine_l : mine_l + 1, :] for axis in range(3)]
            polar = static_ref[mine_d, 6, mine_l : mine_l + 1, :]
            sum_ref[...] = jnp.zeros_like(sum_ref)

            def visit(step, carry, across=across, along=along, at=at, polar=polar):
                dx = step // 3 - 1
                dy = lax.rem(step, 3) - 1
                found = (across + 1 + dx) * rows_y + along + 1 + dy
                shift_x = dx.astype(F32) * HX
                shift_y = dy.astype(F32) * HY
                sums = [sum_ref[axis] for axis in range(3)]
                for dz in (-1, 0, 1):
                    near = [wide_ref[found, item] for item in range(7)]
                    if dz:
                        near = [pltpu.roll(v, (-dz * A) % lanes, 1) for v in near]
                    r0 = at[0] - near[0] - shift_x
                    r1 = at[1] - near[1] - shift_y
                    r2 = at[2] - near[2] - float(dz * HZ)
                    square = r0 * r0 + r1 * r1 + r2 * r2
                    if dz == 0:
                        selfish = own & (step == 4)
                        square = jnp.where(selfish, 1.0, square)
                    inverse = lax.rsqrt(square)
                    inverse_square = inverse * inverse
                    distance = square * inverse
                    root_inverse = lax.rsqrt(polar * near[3])
                    t = 1.0 / (1.0 + (0.5 * BETA) * distance)
                    series = 0.17087277
                    for c in (-0.82215223, 1.48851587, -1.13520398, 0.27886807,
                              -0.18628806, 0.09678418, 0.37409196, 1.00002368, -1.26551223):
                        series = series * t + c
                    bell = jnp.exp((-BETA * BETA) * square)
                    screened = t * jnp.exp(series) * bell * inverse
                    gauss = (2.0 * BETA / ROOT_PI) * bell
                    first = (screened + gauss) * inverse_square
                    second = (3.0 * first + (2.0 * BETA * BETA) * gauss) * inverse_square
                    scaled = THOLE * square * distance * root_inverse
                    damping = jnp.exp(-scaled) * (inverse_square * inverse)
                    first = first - damping
                    second = second - 3.0 * (1.0 + scaled) * damping * inverse_square
                    if dz == 0:
                        first = jnp.where(selfish, 0.0, first)
                        second = jnp.where(selfish, 0.0, second)
                    projected = second * (r0 * near[4] + r1 * near[5] + r2 * near[6])
                    sums[0] = sums[0] + (projected * r0 - first * near[4])
                    sums[1] = sums[1] + (projected * r1 - first * near[5])
                    sums[2] = sums[2] + (projected * r2 - first * near[6])
                for axis in range(3):
                    sum_ref[axis] = sums[axis]
                return carry

            lax.fori_loop(0, 9, visit, 0)
            for axis in range(3):
                out_ref[axis, mine_l : mine_l + 1, :] = jnp.sum(
                    sum_ref[axis], axis=0, keepdims=True
                )


def total_field(far_ref, near_ref, moment, axis):
    field = near_ref[axis] + SELF_GAIN * moment

    def add(d, carry):
        return carry + far_ref[d, axis]

    return field + lax.fori_loop(0, far_ref.shape[0], add, jnp.zeros_like(moment), unroll=8)


def middle_kernel(where_ref, cot_ref, gain_ref, moment_ref, near_ref, far_ref, send_ref):
    cells_x = cot_ref.shape[1]
    devices = far_ref.shape[0]
    gain = gain_ref[...]
    parts = []
    for axis in range(3):
        field = total_field(far_ref, near_ref, moment_ref[where_ref[2], axis], axis)
        cot = jnp.concatenate([cot_ref[axis, cx] for cx in range(cells_x)], axis=0)
        parts.append(gain * (cot + field))
    block = jnp.stack(parts, axis=0)

    def put(d, carry):
        send_ref[d] = block
        return carry

    lax.fori_loop(0, devices, put, 0)


def last_kernel(where_ref, cot_ref, gain_ref, moment_ref, near_ref, far_ref, out_ref):
    cells_x, cells_y = cot_ref.shape[1:3]
    gain = gain_ref[...]
    for axis in range(3):
        field = total_field(far_ref, near_ref, moment_ref[where_ref[2], axis], axis)
        for cx in range(cells_x):
            rows = slice(cx * cells_y, (cx + 1) * cells_y)
            out_ref[axis, cx] = gain[rows] * (cot_ref[axis, cx] + field[rows])


def in_vmem(count, smem_first=False):
    specs = [pl.BlockSpec(memory_space=pltpu.VMEM)] * count
    if smem_first:
        specs[0] = pl.BlockSpec(memory_space=pltpu.SMEM)
    return specs


def call(body, outs, ins, scratch=(), smem_first=False, flops=1000):
    many = isinstance(outs, (list, tuple))
    out_specs = [pl.BlockSpec(memory_space=pltpu.VMEM)] * len(outs) if many else pl.BlockSpec(
        memory_space=pltpu.VMEM
    )
    return pl.pallas_call(
        body,
        out_shape=outs,
        in_specs=in_vmem(len(ins), smem_first),
        out_specs=out_specs,
        scratch_shapes=list(scratch),
        compiler_params=pltpu.CompilerParams(vmem_limit_bytes=VMEM_LIMIT),
        cost_estimate=pl.CostEstimate(flops=flops, bytes_accessed=100000, transcendentals=0),
    )(*ins)


def green_values(grid_x, grid_y, grid_z, length_x, length_y, length_z):
    def part(grid, length):
        signed = jnp.where(2 * grid < length, grid, grid - length).astype(F32) / length
        angle = 2.0 * math.pi / length * grid.astype(F32)
        factor = 9.0 / ((2.0 + jnp.cos(angle)) * (2.0 + jnp.cos(angle)))
        return (signed * signed, factor)

    square_x, factor_x = part(grid_x, length_x)
    square_y, factor_y = part(grid_y, length_y)
    square_z, factor_z = part(grid_z, length_z)
    square = square_x + square_y + square_z
    anchor = (grid_x == 0) & (grid_y == 0) & (grid_z == 0)
    safe = jnp.where(anchor, 1.0, square)
    value = jnp.exp(-(math.pi / BETA) * (math.pi / BETA) * safe) / (math.pi * safe)
    value = value * factor_x * factor_y * factor_z / (length_x * length_y * length_z)
    return jnp.where(anchor | (grid_z >= length_z), 0.0, value)


def shards(cotangent, polarizability, site_offset, site_fraction, cell_count):
    _, cells_x, cells_y, lanes = cotangent.shape
    layers = cell_count.shape[2]
    devices_x = lax.axis_size("gx")
    devices_y = lax.axis_size("gy")
    devices = devices_x * devices_y
    columns = cells_x * cells_y
    total_x = devices_x * cells_x
    length_x = total_x * HX
    length_y = devices_y * cells_y * HY
    length_z = layers * HZ
    index_x = lax.axis_index("gx")
    index_y = lax.axis_index("gy")
    me = index_x * devices_y + index_y
    where = jnp.stack([index_x, index_y, me]).astype(jnp.int32)

    def exchange(value):
        return lax.all_to_all(value, AXES, split_axis=0, concat_axis=0, tiled=True)

    send, gain = call(
        pack_kernel,
        [
            jax.ShapeDtypeStruct((devices, 7, columns, lanes), F32),
            jax.ShapeDtypeStruct((columns, lanes), F32),
        ],
        [cotangent, polarizability, site_offset, site_fraction, cell_count],
    )
    static = exchange(send)

    modes = me * MODES + jnp.arange(MODES, dtype=jnp.int32)
    mode_rows = jnp.broadcast_to(modes[:, None], (MODES, lanes))
    order = jnp.arange(4, dtype=jnp.int32)[:, None]
    angle = (2.0 * math.pi / length_z) * (modes[None, :] * order % length_z).astype(F32)
    phase = jnp.concatenate(
        [jnp.cos(angle) + jnp.sin(angle), jnp.cos(angle) - jnp.sin(angle)], axis=0
    )
    phase = jnp.broadcast_to(phase[:, :, None], (8, MODES, lanes))
    green = green_values(
        jnp.arange(length_x, dtype=jnp.int32)[None, None, :],
        jnp.arange(length_y, dtype=jnp.int32)[None, :, None],
        modes[:, None, None],
        length_x,
        length_y,
        length_z,
    ).reshape(MODES * length_y, length_x)
    forward, inverse = x_tables(total_x, length_x)
    y_high, y_low = two_terms(cas_table(length_y))
    y_table = np.concatenate([y_high, y_low, y_high], axis=1)

    tall = length_y * MODES
    kept = devices if devices * columns <= 256 else 1
    far_scratch = [
        pltpu.VMEM((total_x // 4, tall + 3 * MODES, 4 * 2 * SPAN), F32),
        pltpu.VMEM((length_x // 128, tall, 128), F32),
        pltpu.VMEM((length_x // 128, tall, 128), F32),
        pltpu.VMEM((total_x // 2, tall + 32, 2 * 4 * SPAN), BF16),
        pltpu.VMEM((kept, columns, 2 * SPAN, 2 * lanes), BF16),
        pltpu.VMEM((kept, columns, 2 * SPAN, lanes), F32),
        pltpu.VMEM((kept, columns, 2 * MODES, lanes), F32),
    ]
    far = functools.partial(far_kernel, (devices_x, devices_y, cells_x, cells_y, length_z))
    near = functools.partial(near_kernel, (devices_x, devices_y, cells_x, cells_y))
    near_scratch = [
        pltpu.VMEM(((cells_x + 2) * (cells_y + 2) * 7 * A, lanes), F32),
        pltpu.VMEM(((cells_x + 2) * (cells_y + 2), 7, A, lanes), F32),
        pltpu.VMEM((3, A, lanes), F32),
    ]
    moment = static[:, 3:6]
    for turn in range(ITERS):
        partial = call(
            far,
            jax.ShapeDtypeStruct((devices, 3, columns, lanes), F32),
            [
                static,
                moment,
                mode_rows,
                phase,
                green,
                *(jnp.asarray(t) for t in forward),
                *(jnp.asarray(t) for t in inverse),
                jnp.asarray(y_table),
            ],
            far_scratch,
            flops=10**9,
        )
        partial = exchange(partial)
        close = call(
            near,
            jax.ShapeDtypeStruct((3, columns, lanes), F32),
            [where, static, moment],
            near_scratch,
            smem_first=True,
            flops=10**8,
        )
        ins = [where, cotangent, gain, moment, close, partial]
        if turn < ITERS - 1:
            send = call(
                middle_kernel,
                jax.ShapeDtypeStruct((devices, 3, columns, lanes), F32),
                ins,
                smem_first=True,
            )
            moment = exchange(send)
        else:
            moment = call(
                last_kernel,
                jax.ShapeDtypeStruct(cotangent.shape, F32),
                ins,
                smem_first=True,
            )
    return moment


def solution(mesh):
    return jax.shard_map(
        shards,
        mesh=mesh,
        in_specs=(
            P(None, "gx", "gy", None),
            P("gx", "gy", None),
            P(None, "gx", "gy", None),
            P(None, "gx", "gy", None),
            P("gx", "gy", None),
        ),
        out_specs=P(None, "gx", "gy", None),
        check_vma=False,
    )
```

profile of v0, /device:TPU:0, one launch (start us, length us, event | category | flops | bytes accessed | tf_op | source)
XLA Modules:
  0.0 118.4 jit_solution(17953092601067253223)
XLA Ops:
  0.0 1.8 %shard_map.100 = (f32[32,7,4,128]{3,2,1,0:T(4,128)}, f32[4,128]{1,0:T(4,128)}) custom-call(f32[3,2,2,128]{3,2,1,0:T(2,128)} %cot_ref.5, f32[2,2,128]{2,1,0:T(2,128)} %polar_ref.1, s32[3,2,2,128]{3,2,1,0:T(2,128)} %offset_ref.1, f32[3,2,2,128]{3,2,1,0:T(2,128)} %fraction_ref.1, s32[2,2,16]{2,1,0:T(2,128)} %count_ref.1), custom_call_target="tpu_custom_call" | custom-call | flops 1000 | bytes 100000 | tf_op jit(solution)/shard_map/pallas_call | solution.py:468
  1.8 7.3 %all-to-all-start = ((f32[32,7,4,128]{3,2,1,0:T(4,128)}), f32[32,7,4,128]{3,2,1,0:T(4,128)S(1)}, u32[]{:S(2)}, u32[]{:S(2)}) async-start(f32[32,7,4,128]{3,2,1,0:T(4,128)} %get-tuple-element.8), calls=%async_computation | async-start | bytes 917504 | tf_op jit(solution)/shard_map/all_to_all | solution.py:514
  9.4 0.1 add.132
  9.4 0.1 add.133
  9.5 0.1 mul.215
  9.6 0.1 mul.216
  9.7 0.1 and.51
  9.7 0.1 and.52
  9.8 0.1 or.13
  9.9 0.1 or.14
  10.0 0.1 mul.210
  10.1 0.1 broadcast_and_fusion
  10.1 0.1 broadcast_add_fusion
  10.2 1.1 fusion.9.green_ref
  11.4 10.8 %all-to-all-done.static_ref.place_ref = f32[32,7,4,128]{3,2,1,0:T(4,128)S(1)} async-done(((f32[32,7,4,128]{3,2,1,0:T(4,128)}), f32[32,7,4,128]{3,2,1,0:T(4,128)S(1)}, u32[]{:S(2)}, u32[]{:S(2)}) %all-to-all-start) | async-done | bytes 458784 | tf_op jit(solution)/shard_map/all_to_all | solution.py:514
  22.2 0.7 slice.4.moment_ref
  23.0 0.7 broadcast_in_dim.11.phase_ref
  23.7 0.7 broadcast_in_dim.10.mode_ref
  24.3 24.9 %shard_map.102 = f32[32,3,4,128]{3,2,1,0:T(4,128)} custom-call(f32[32,7,4,128]{3,2,1,0:T(4,128)} %copy-done, f32[32,3,4,128]{3,2,1,0:T(4,128)} %slice.4.moment_ref, s32[8,128]{1,0:T(8,128)} %broadcast_in_dim.10.mode_ref, f32[8,8,128]{2,1,0:T(8,128)} %broadcast_in_dim.11.phase_ref, f32[512,128]{1,0:T(8,128)} %fusion.9.green_ref, ...), custom_call_target="tpu_custom_call" | custom-call | flops 1000000000 | bytes 100000 | tf_op jit(solution)/shard_map/pallas_call | solution.py:468
  49.3 4.0 %all-to-all-start.1 = ((f32[32,3,4,128]{3,2,1,0:T(4,128)}), f32[32,3,4,128]{3,2,1,0:T(4,128)S(1)}, u32[]{:S(2)}, u32[]{:S(2)}) async-start(f32[32,3,4,128]{3,2,1,0:T(4,128)} %shard_map.102), calls=%async_computation.1 | async-start | bytes 393216 | tf_op jit(solution)/shard_map/all_to_all | solution.py:514
  53.2 0.7 pad_add_fusion.where_ref
  53.9 7.1 %shard_map.101.near_ref = f32[3,4,128]{2,1,0:T(4,128)} custom-call(s32[3]{0:T(128)} %pad_add_fusion.where_ref, f32[32,7,4,128]{3,2,1,0:T(4,128)} %copy-done, f32[32,3,4,128]{3,2,1,0:T(4,128)} %slice.4.moment_ref), custom_call_target="tpu_custom_call" | custom-call | flops 100000000 | bytes 100000 | tf_op jit(solution)/shard_map/pallas_call | solution.py:468
  61.0 1.5 %all-to-all-done.1.far_ref = f32[32,3,4,128]{3,2,1,0:T(4,128)S(1)} async-done(((f32[32,3,4,128]{3,2,1,0:T(4,128)}), f32[32,3,4,128]{3,2,1,0:T(4,128)S(1)}, u32[]{:S(2)}, u32[]{:S(2)}) %all-to-all-start.1) | async-done | bytes 196640 | tf_op jit(solution)/shard_map/all_to_all | solution.py:514
  62.6 0.7 copy-done.2
  63.3 2.1 %shard_map.103 = f32[32,3,4,128]{3,2,1,0:T(4,128)} custom-call(s32[3]{0:T(128)} %pad_add_fusion.where_ref, f32[3,2,2,128]{3,2,1,0:T(2,128)} %cot_ref.5, f32[4,128]{1,0:T(4,128)} %get-tuple-element.7.gain_ref, f32[32,3,4,128]{3,2,1,0:T(4,128)} %slice.4.moment_ref, f32[3,4,128]{2,1,0:T(4,128)} %shard_map.101.near_ref, f32[32,3,4,128]{3,2,1,0:T(4,128)} %copy-done.2), custom_call_target="tpu_custom_call" | custom-call | flops 1000 | bytes 100000 | tf_op jit(solution)/shard_map/pallas_call | solution.py:468
  65.3 13.8 %all_to_all.20.moment_ref = f32[32,3,4,128]{3,2,1,0:T(4,128)} all-to-all(f32[32,3,4,128]{3,2,1,0:T(4,128)} %shard_map.103), channel_id=1, replica_groups=mesh['gx'=8,'gy'=4] {'gx','gy'}, dimensions={0} | all-to-all | bytes 393216 | tf_op jit(solution)/shard_map/all_to_all | solution.py:514
  79.1 24.9 %shard_map.105 = f32[32,3,4,128]{3,2,1,0:T(4,128)} custom-call(f32[32,7,4,128]{3,2,1,0:T(4,128)} %copy-done, f32[32,3,4,128]{3,2,1,0:T(4,128)} %all_to_all.20.moment_ref, s32[8,128]{1,0:T(8,128)} %broadcast_in_dim.10.mode_ref, f32[8,8,128]{2,1,0:T(8,128)} %broadcast_in_dim.11.phase_ref, f32[512,128]{1,0:T(8,128)} %fusion.9.green_ref, ...), custom_call_target="tpu_custom_call" | custom-call | flops 1000000000 | bytes 100000 | tf_op jit(solution)/shard_map/pallas_call | solution.py:468
  104.0 2.6 %all-to-all-start.3 = ((f32[32,3,4,128]{3,2,1,0:T(4,128)}), f32[32,3,4,128]{3,2,1,0:T(4,128)S(1)}, u32[]{:S(2)}, u32[]{:S(2)}) async-start(f32[32,3,4,128]{3,2,1,0:T(4,128)} %shard_map.105), calls=%async_computation.3 | async-start | bytes 393216 | tf_op jit(solution)/shard_map/all_to_all | solution.py:514
  106.6 7.2 %shard_map.104.near_ref = f32[3,4,128]{2,1,0:T(4,128)} custom-call(s32[3]{0:T(128)} %pad_add_fusion.where_ref, f32[32,7,4,128]{3,2,1,0:T(4,128)} %copy-done, f32[32,3,4,128]{3,2,1,0:T(4,128)} %all_to_all.20.moment_ref), custom_call_target="tpu_custom_call" | custom-call | flops 100000000 | bytes 100000 | tf_op jit(solution)/shard_map/pallas_call | solution.py:468
  113.7 2.2 %all-to-all-done.3.far_ref = f32[32,3,4,128]{3,2,1,0:T(4,128)S(1)} async-done(((f32[32,3,4,128]{3,2,1,0:T(4,128)}), f32[32,3,4,128]{3,2,1,0:T(4,128)S(1)}, u32[]{:S(2)}, u32[]{:S(2)}) %all-to-all-start.3) | async-done | bytes 196640 | tf_op jit(solution)/shard_map/all_to_all | solution.py:514
  115.9 0.7 copy-done.1
  116.6 1.8 %shard_map.106 = f32[3,2,2,128]{3,2,1,0:T(2,128)} custom-call(s32[3]{0:T(128)} %pad_add_fusion.where_ref, f32[3,2,2,128]{3,2,1,0:T(2,128)} %cot_ref.5, f32[4,128]{1,0:T(4,128)} %get-tuple-element.7.gain_ref, f32[32,3,4,128]{3,2,1,0:T(4,128)} %all_to_all.20.moment_ref, f32[3,4,128]{2,1,0:T(4,128)} %shard_map.104.near_ref, f32[32,3,4,128]{3,2,1,0:T(4,128)} %copy-done.1), custom_call_target="tpu_custom_call" | custom-call | flops 1000 | bytes 100000 | tf_op jit(solution)/shard_map/pallas_call | solution.py:468
  (16 shorter events, 0.3 us)
Async XLA Ops:
  1.8 20.4 %all-to-all-start = ((f32[32,7,4,128]{3,2,1,0:T(4,128)}), f32[32,7,4,128]{3,2,1,0:T(4,128)S(1)}, u32[]{:S(2)}, u32[]{:S(2)}) async-start(f32[32,7,4,128]{3,2,1,0:T(4,128)} %get-tuple-element.8), calls=%async_computation | async-start | bytes 917504 | tf_op jit(solution)/shard_map/all_to_all | solution.py:514
  22.2 2.1 %copy-start = (f32[32,7,4,128]{3,2,1,0:T(4,128)}, f32[32,7,4,128]{3,2,1,0:T(4,128)S(1)}, u32[]{:S(2)}) copy-start(f32[32,7,4,128]{3,2,1,0:T(4,128)S(1)} %all-to-all-done.static_ref.place_ref) | copy-start | bytes 1376260
  49.3 13.3 %all-to-all-start.1 = ((f32[32,3,4,128]{3,2,1,0:T(4,128)}), f32[32,3,4,128]{3,2,1,0:T(4,128)S(1)}, u32[]{:S(2)}, u32[]{:S(2)}) async-start(f32[32,3,4,128]{3,2,1,0:T(4,128)} %shard_map.102), calls=%async_computation.1 | async-start | bytes 393216 | tf_op jit(solution)/shard_map/all_to_all | solution.py:514
  62.6 0.7 copy-start.2
  104.0 11.9 %all-to-all-start.3 = ((f32[32,3,4,128]{3,2,1,0:T(4,128)}), f32[32,3,4,128]{3,2,1,0:T(4,128)S(1)}, u32[]{:S(2)}, u32[]{:S(2)}) async-start(f32[32,3,4,128]{3,2,1,0:T(4,128)} %shard_map.105), calls=%async_computation.3 | async-start | bytes 393216 | tf_op jit(solution)/shard_map/all_to_all | solution.py:514
  115.9 0.7 copy-start.1
where the time goes:
time: 119 us; the launch traced here: 118 us
  Pallas kernels  69.8 us (59%)
  waiting for transfers between devices  14.5 us (12%)
  starting transfers between devices  13.8 us (12%)
  blocking collectives  13.8 us (12%)
  local copies, waits for them, and re-layouts  4.15 us (3%)
  other arithmetic  2.19 us (2%)
    pallas_call x7, Pallas kernels, call(): pl.pallas_call(body, out_shape=outs, in_specs=in_vmem(len(ins), smem_firs...  69.8 us
    all_to_all x3, waiting for transfers between devices, exchange(): return lax.all_to_all(value, AXES, split_axis=0, concat_axis=0, tiled=True)  14.5 us
    all_to_all x3, starting transfers between devices, exchange(): return lax.all_to_all(value, AXES, split_axis=0, concat_axis=0, tiled=True)  13.8 us
    all_to_all x1, blocking collectives, exchange(): return lax.all_to_all(value, AXES, split_axis=0, concat_axis=0, tiled=True)  13.8 us
  transfers between devices with their start and end apart: 3, of which 3 were waited for; matrix products, arithmetic and copies ran while one was open for 2% of the time, Pallas kernels for 12%

commit v1 on v0

--- a/solution.py
+++ b/solution.py
@@ -20,11 +20,12 @@
 ROOT_PI = 1.7724538509055159
 SELF_GAIN = 4.0 * BETA * BETA * BETA / (3.0 * ROOT_PI)
 MODES = 8
+STATIC_UNROLL = 2
 SPAN = 16
 AXES = ("gx", "gy")
 F32 = jnp.float32
 BF16 = jnp.bfloat16
-VMEM_LIMIT = 56 * 1024 * 1024
+MIB = 1024 * 1024
 
 
 def two_terms(table):
@@ -105,7 +106,7 @@
     return 1.0 - 2.0 * sine * sine, 2.0 * sine * cosine
 
 
-def pack_kernel(cot_ref, polar_ref, offset_ref, fraction_ref, count_ref, send_ref, gain_ref):
+def pack_kernel(cot_ref, polar_ref, offset_ref, fraction_ref, count_ref, send_ref, gain_ref, own_ref):
     cells_x, cells_y, lanes = polar_ref.shape
     devices = send_ref.shape[0]
     cells = lanes // A
@@ -126,6 +127,7 @@
         rows[6].append(polar_ref[cx])
     gain_ref[...] = jnp.concatenate(gains, axis=0)
     block = jnp.stack([jnp.concatenate(parts, axis=0) for parts in rows], axis=0)
+    own_ref[...] = block[3:6]
 
     def put(d, carry):
         send_ref[d] = block
@@ -136,10 +138,10 @@
 
 def far_kernel(
     shape,
+    lead,
+    where_ref,
     place_ref,
     moment_ref,
-    mode_ref,
-    phase_ref,
     green_ref,
     fx_high_ref,
     fx_low_ref,
@@ -149,7 +151,6 @@
     out_ref,
     cell_ref,
     line_ref,
-    back_ref,
     wave_ref,
     side_ref,
     rise_ref,
@@ -166,40 +167,50 @@
     per_cell = HY * MODES
     turn_x = 4 // cells_x
     keep = side_ref.shape[0] > 1
+    unroll = min(4, devices_y)
     layer = (lax.broadcasted_iota(jnp.int32, (1, lanes), 1) // A) * HZ
+    mode = where_ref[2] * MODES + lax.broadcasted_iota(jnp.int32, (MODES, lanes), 0)
+    plus, minus = [], []
+    for order in range(4):
+        cosine, sine = turns(lax.rem(mode * order, points_z), points_z)
+        plus.append(cosine + sine)
+        minus.append(cosine - sine)
     cell_ref[...] = jnp.zeros_like(cell_ref)
 
-    def statics(d, l):
+    def statics(d):
         k = d if keep else 0
-        place = [place_ref[d, axis, l : l + 1, :] for axis in range(3)]
+        place = [place_ref[d, axis] for axis in range(3)]
         whole = [jnp.floor(value) for value in place]
         parts = [spline(value - low) for value, low in zip(place, whole)]
-        anchor = [low.astype(jnp.int32) - 1 for low in whole]
-        values_x = basis(anchor[0], parts[0][0])
-        slopes_x = basis(anchor[0], parts[0][1])
-        side = jnp.concatenate([slopes_x, values_x], axis=1)
-        high, low = split(side)
-        side_ref[k, l] = jnp.concatenate([high, low], axis=0)
-        rise_ref[k, l] = jnp.concatenate(
-            [basis(anchor[1], parts[1][0]), basis(anchor[1], parts[1][1])], axis=0
-        )
-        phase = lax.rem(mode_ref[...] * (anchor[2] + layer), points_z)
-        cosine, sine = turns(phase, points_z)
-        found = []
-        for weights in parts[2]:
-            plus = weights[0] * phase_ref[0]
-            minus = weights[0] * phase_ref[4]
-            for order in range(1, 4):
-                plus = plus + weights[order] * phase_ref[order]
-                minus = minus + weights[order] * phase_ref[4 + order]
-            found.append(cosine * plus + sine * minus)
-        edge_ref[k, l] = jnp.concatenate(found, axis=0)
+        anchors = [low.astype(jnp.int32) - 1 for low in whole]
+        for l in range(columns):
+            row = slice(l, l + 1)
+            anchor = [value[row] for value in anchors]
+            weights = [[[v[row] for v in kind] for kind in part] for part in parts]
+            slopes_x = basis(anchor[0], weights[0][1])
+            values_x = basis(anchor[0], weights[0][0])
+            side = jnp.concatenate([slopes_x, values_x], axis=1)
+            high, low = split(side)
+            side_ref[k, l] = jnp.concatenate([high, low], axis=0)
+            rise_ref[k, l] = jnp.concatenate(
+                [basis(anchor[1], weights[1][0]), basis(anchor[1], weights[1][1])], axis=0
+            )
+            cosine, sine = turns(lax.rem(mode * (anchor[2] + layer), points_z), points_z)
+            found = []
+            for kind in weights[2]:
+                up = kind[0] * plus[0]
+                down = kind[0] * minus[0]
+                for order in range(1, 4):
+                    up = up + kind[order] * plus[order]
+                    down = down + kind[order] * minus[order]
+                found.append(cosine * up + sine * down)
+            edge_ref[k, l] = jnp.concatenate(found, axis=0)
 
     def spread(d, l, slot, group, start):
         k = d if keep else 0
-        first = edge_ref[k, l, :MODES] * moment_ref[d, 0, l : l + 1, :]
-        second = edge_ref[k, l, :MODES] * moment_ref[d, 1, l : l + 1, :]
-        third = edge_ref[k, l, MODES:] * moment_ref[d, 2, l : l + 1, :]
+        first = edge_ref[k, l, :MODES] * moment_ref[d, lead, l : l + 1, :]
+        second = edge_ref[k, l, :MODES] * moment_ref[d, lead + 1, l : l + 1, :]
+        third = edge_ref[k, l, MODES:] * moment_ref[d, lead + 2, l : l + 1, :]
         tiles = []
         for y in range(HY + 3):
             value = rise_ref[k, l, y : y + 1, :]
@@ -219,14 +230,21 @@
         got = (got[:, 0] + got[:, 1]).reshape(reach, got.shape[3])
         cell_ref[group, pl.ds(start, reach), :] = cell_ref[group, pl.ds(start, reach), :] + got
 
+    def prepare(d, carry):
+        statics(d)
+        return carry
+
+    if keep:
+        lax.fori_loop(0, devices_x * devices_y, prepare, 0, unroll=STATIC_UNROLL)
+
     def spread_row(pair, carry):
         for odd in range(turn_x):
             gx = pair * turn_x + odd
 
             def spread_device(gy, inner):
                 d = gx * devices_y + gy
-                for l in range(columns):
-                    statics(d, l)
+                if not keep:
+                    statics(d)
                 for l in range(columns):
                     slot = odd * cells_x + l // cells_y
                     start = pl.multiple_of(
@@ -235,19 +253,26 @@
                     spread(d, l, slot, pair, start)
                 return inner
 
-            lax.fori_loop(0, devices_y, spread_device, 0)
+            lax.fori_loop(0, devices_y, spread_device, 0, unroll=unroll)
         return carry
 
     lax.fori_loop(0, devices_x // turn_x, spread_row, 0)
 
     cell_ref[:, :spill, :] = cell_ref[:, :spill, :] + cell_ref[:, tall : tall + spill, :]
     total = jnp.zeros((tall, length_x), F32)
-    for group in range(cell_ref.shape[0]):
-        high, low = split(cell_ref[group, :tall, :])
-        total = total + (
-            dot(high, fx_high_ref[group])
-            + dot(low, fx_high_ref[group])
-            + dot(high, fx_low_ref[group])
+    for group in range(0, cell_ref.shape[0], 2):
+        one_high, one_low = split(cell_ref[group, :tall, :])
+        two_high, two_low = split(cell_ref[group + 1, :tall, :])
+        one, two = fx_high_ref[group], fx_high_ref[group + 1]
+        total = total + dot(
+            jnp.concatenate([one_high, one_low], axis=1), jnp.concatenate([one, one], axis=0)
+        )
+        total = total + dot(
+            jnp.concatenate([two_high, two_low], axis=1), jnp.concatenate([two, two], axis=0)
+        )
+        total = total + dot(
+            jnp.concatenate([one_high, two_high], axis=1),
+            jnp.concatenate([fx_low_ref[group], fx_low_ref[group + 1]], axis=0),
         )
     blocks = length_x // line_ref.shape[2]
     width = line_ref.shape[2]
@@ -258,25 +283,32 @@
         high, low = split(value)
         return dot(y_ref[...], jnp.concatenate([high, high, low], axis=0))
 
-    for mode in range(MODES):
-        for block in range(blocks):
-            got = along_y(line_ref[block, pl.ds(mode, length_y, stride=MODES), :])
-            got = got * green_ref[
-                mode * length_y : (mode + 1) * length_y, block * width : (block + 1) * width
-            ]
-            back_ref[block, pl.ds(mode, length_y, stride=MODES), :] = along_y(got)
-    high, low = split(jnp.concatenate([back_ref[block] for block in range(blocks)], axis=1))
-    lane = lax.broadcasted_iota(jnp.int32, (tall, 2 * 4 * SPAN), 1)
+    for block in range(blocks):
+        found = []
+        for number in range(MODES):
+            got = along_y(line_ref[block, pl.ds(number, length_y, stride=MODES), :])
+            found.append(
+                got
+                * green_ref[
+                    number * length_y : (number + 1) * length_y,
+                    block * width : (block + 1) * width,
+                ]
+            )
+        for number in range(MODES):
+            line_ref[block, pl.ds(number, length_y, stride=MODES), :] = along_y(found[number])
+    high, low = split(jnp.concatenate([line_ref[block] for block in range(blocks)], axis=1))
+    both = jnp.concatenate([high, low], axis=1)
+    lane = lax.broadcasted_iota(jnp.int32, (tall, 4 * 4 * SPAN), 1)
     rest = lane // SPAN % 2 == 1
-    for group in range(wave_ref.shape[0]):
-        got = (
-            dot(high, ix_high_ref[group])
-            + dot(low, ix_high_ref[group])
-            + dot(high, ix_low_ref[group])
-        )
+    for group in range(0, wave_ref.shape[0], 2):
+        one = jnp.concatenate([ix_high_ref[group], ix_high_ref[group + 1]], axis=1)
+        two = jnp.concatenate([ix_low_ref[group], ix_low_ref[group + 1]], axis=1)
+        got = dot(both, jnp.concatenate([one, one], axis=0)) + dot(high, two)
         got = jnp.where(rest, got - got.astype(BF16).astype(F32), got).astype(BF16)
-        wave_ref[group, :tall, :] = got
-        wave_ref[group, tall:, :] = got[: wave_ref.shape[1] - tall]
+        for odd in range(2):
+            part = got[:, odd * 8 * SPAN : (odd + 1) * 8 * SPAN]
+            wave_ref[group + odd, :tall, :] = part
+            wave_ref[group + odd, tall:, :] = part[: wave_ref.shape[1] - tall]
 
     window = -(-reach // 16) * 16
 
@@ -299,29 +331,33 @@
             sums[2] = sums[2] + plain * value
         value = edge_ref[k, l, :MODES]
         slope = edge_ref[k, l, MODES:]
-        for axis, part in enumerate((value, value, slope)):
-            out_ref[d, axis, l : l + 1, :] = -jnp.sum(sums[axis] * part, axis=0, keepdims=True)
+        return [
+            -jnp.sum(sums[axis] * part, axis=0, keepdims=True)
+            for axis, part in enumerate((value, value, slope))
+        ]
 
     def gather_row(gx, carry):
         def gather_device(gy, inner):
             d = gx * devices_y + gy
             if not keep:
-                for l in range(columns):
-                    statics(d, l)
+                statics(d)
+            found = []
             for l in range(columns):
                 across = l // cells_y
                 start = pl.multiple_of((gy * cells_y + l % cells_y) * per_cell, per_cell)
                 group = (gx * cells_x + across - across % 2) // 2
-                gather(d, l, across % 2, group, start)
+                found.append(gather(d, l, across % 2, group, start))
+            for axis in range(3):
+                out_ref[d, axis] = jnp.concatenate([part[axis] for part in found], axis=0)
             return inner
 
-        lax.fori_loop(0, devices_y, gather_device, 0)
+        lax.fori_loop(0, devices_y, gather_device, 0, unroll=unroll)
         return carry
 
     lax.fori_loop(0, devices_x, gather_row, 0)
 
 
-def near_kernel(shape, where_ref, static_ref, moment_ref, out_ref, raw_ref, wide_ref, sum_ref):
+def near_kernel(shape, lead, where_ref, static_ref, moment_ref, out_ref, raw_ref, wide_ref, sum_ref):
     devices_x, devices_y, cells_x, cells_y = shape
     lanes = static_ref.shape[3]
     rows_x, rows_y = cells_x + 2, cells_y + 2
@@ -339,7 +375,7 @@
                 if item < 4:
                     row = static_ref[d, item if item < 3 else 6, pl.ds(l, 1), :]
                 else:
-                    row = moment_ref[d, item - 4, pl.ds(l, 1), :]
+                    row = moment_ref[d, lead + item - 4, pl.ds(l, 1), :]
                 first = ((a * rows_y + b) * 7 + item) * A
                 raw_ref[first : first + A, :] = jnp.where(own, row, 0.0)
     group = lax.broadcasted_iota(jnp.int32, (lanes, lanes), 0) // A
@@ -425,16 +461,17 @@
     return field + lax.fori_loop(0, far_ref.shape[0], add, jnp.zeros_like(moment), unroll=8)
 
 
-def middle_kernel(where_ref, cot_ref, gain_ref, moment_ref, near_ref, far_ref, send_ref):
+def middle_kernel(cot_ref, gain_ref, moment_ref, near_ref, far_ref, send_ref, own_ref):
     cells_x = cot_ref.shape[1]
     devices = far_ref.shape[0]
     gain = gain_ref[...]
     parts = []
     for axis in range(3):
-        field = total_field(far_ref, near_ref, moment_ref[where_ref[2], axis], axis)
+        field = total_field(far_ref, near_ref, moment_ref[axis], axis)
         cot = jnp.concatenate([cot_ref[axis, cx] for cx in range(cells_x)], axis=0)
         parts.append(gain * (cot + field))
     block = jnp.stack(parts, axis=0)
+    own_ref[...] = block
 
     def put(d, carry):
         send_ref[d] = block
@@ -443,11 +480,11 @@
     lax.fori_loop(0, devices, put, 0)
 
 
-def last_kernel(where_ref, cot_ref, gain_ref, moment_ref, near_ref, far_ref, out_ref):
+def last_kernel(cot_ref, gain_ref, moment_ref, near_ref, far_ref, out_ref):
     cells_x, cells_y = cot_ref.shape[1:3]
     gain = gain_ref[...]
     for axis in range(3):
-        field = total_field(far_ref, near_ref, moment_ref[where_ref[2], axis], axis)
+        field = total_field(far_ref, near_ref, moment_ref[axis], axis)
         for cx in range(cells_x):
             rows = slice(cx * cells_y, (cx + 1) * cells_y)
             out_ref[axis, cx] = gain[rows] * (cot_ref[axis, cx] + field[rows])
@@ -460,7 +497,7 @@
     return specs
 
 
-def call(body, outs, ins, scratch=(), smem_first=False, flops=1000):
+def call(body, outs, ins, scratch=(), smem_first=False, flops=1000, limit=12):
     many = isinstance(outs, (list, tuple))
     out_specs = [pl.BlockSpec(memory_space=pltpu.VMEM)] * len(outs) if many else pl.BlockSpec(
         memory_space=pltpu.VMEM
@@ -471,7 +508,7 @@
         in_specs=in_vmem(len(ins), smem_first),
         out_specs=out_specs,
         scratch_shapes=list(scratch),
-        compiler_params=pltpu.CompilerParams(vmem_limit_bytes=VMEM_LIMIT),
+        compiler_params=pltpu.CompilerParams(vmem_limit_bytes=limit * MIB),
         cost_estimate=pl.CostEstimate(flops=flops, bytes_accessed=100000, transcendentals=0),
     )(*ins)
 
@@ -513,24 +550,21 @@
     def exchange(value):
         return lax.all_to_all(value, AXES, split_axis=0, concat_axis=0, tiled=True)
 
-    send, gain = call(
+    own_shape = jax.ShapeDtypeStruct((3, columns, lanes), F32)
+    moment_shape = jax.ShapeDtypeStruct((devices, 3, columns, lanes), F32)
+    send, gain, own = call(
         pack_kernel,
         [
             jax.ShapeDtypeStruct((devices, 7, columns, lanes), F32),
             jax.ShapeDtypeStruct((columns, lanes), F32),
+            own_shape,
         ],
         [cotangent, polarizability, site_offset, site_fraction, cell_count],
+        limit=58,
     )
     static = exchange(send)
 
     modes = me * MODES + jnp.arange(MODES, dtype=jnp.int32)
-    mode_rows = jnp.broadcast_to(modes[:, None], (MODES, lanes))
-    order = jnp.arange(4, dtype=jnp.int32)[:, None]
-    angle = (2.0 * math.pi / length_z) * (modes[None, :] * order % length_z).astype(F32)
-    phase = jnp.concatenate(
-        [jnp.cos(angle) + jnp.sin(angle), jnp.cos(angle) - jnp.sin(angle)], axis=0
-    )
-    phase = jnp.broadcast_to(phase[:, :, None], (8, MODES, lanes))
     green = green_values(
         jnp.arange(length_x, dtype=jnp.int32)[None, None, :],
         jnp.arange(length_y, dtype=jnp.int32)[None, :, None],
@@ -548,62 +582,54 @@
     far_scratch = [
         pltpu.VMEM((total_x // 4, tall + 3 * MODES, 4 * 2 * SPAN), F32),
         pltpu.VMEM((length_x // 128, tall, 128), F32),
-        pltpu.VMEM((length_x // 128, tall, 128), F32),
         pltpu.VMEM((total_x // 2, tall + 32, 2 * 4 * SPAN), BF16),
         pltpu.VMEM((kept, columns, 2 * SPAN, 2 * lanes), BF16),
         pltpu.VMEM((kept, columns, 2 * SPAN, lanes), F32),
         pltpu.VMEM((kept, columns, 2 * MODES, lanes), F32),
     ]
-    far = functools.partial(far_kernel, (devices_x, devices_y, cells_x, cells_y, length_z))
-    near = functools.partial(near_kernel, (devices_x, devices_y, cells_x, cells_y))
+    far_shape = (devices_x, devices_y, cells_x, cells_y, length_z)
+    near_shape = (devices_x, devices_y, cells_x, cells_y)
+
+    def far_first(where_ref, static_ref, *rest):
+        far_kernel(far_shape, 3, where_ref, static_ref, static_ref, *rest)
+
+    def near_first(where_ref, static_ref, *rest):
+        near_kernel(near_shape, 3, where_ref, static_ref, static_ref, *rest)
+
+    far_later = functools.partial(far_kernel, far_shape, 0)
+    near_later = functools.partial(near_kernel, near_shape, 0)
     near_scratch = [
         pltpu.VMEM(((cells_x + 2) * (cells_y + 2) * 7 * A, lanes), F32),
         pltpu.VMEM(((cells_x + 2) * (cells_y + 2), 7, A, lanes), F32),
         pltpu.VMEM((3, A, lanes), F32),
     ]
-    moment = static[:, 3:6]
+    tables = [green, *(jnp.asarray(t) for t in (*forward, *inverse, y_table))]
+    data = [where, static]
     for turn in range(ITERS):
         partial = call(
-            far,
-            jax.ShapeDtypeStruct((devices, 3, columns, lanes), F32),
-            [
-                static,
-                moment,
-                mode_rows,
-                phase,
-                green,
-                *(jnp.asarray(t) for t in forward),
-                *(jnp.asarray(t) for t in inverse),
-                jnp.asarray(y_table),
-            ],
+            far_later if turn else far_first,
+            moment_shape,
+            data + tables,
             far_scratch,
+            smem_first=True,
             flops=10**9,
+            limit=20 if kept > 1 else 58,
         )
         partial = exchange(partial)
         close = call(
-            near,
-            jax.ShapeDtypeStruct((3, columns, lanes), F32),
-            [where, static, moment],
+            near_later if turn else near_first,
+            own_shape,
+            data,
             near_scratch,
             smem_first=True,
             flops=10**8,
         )
-        ins = [where, cotangent, gain, moment, close, partial]
+        ins = [cotangent, gain, own, close, partial]
         if turn < ITERS - 1:
-            send = call(
-                middle_kernel,
-                jax.ShapeDtypeStruct((devices, 3, columns, lanes), F32),
-                ins,
-                smem_first=True,
-            )
-            moment = exchange(send)
+            send, own = call(middle_kernel, [moment_shape, own_shape], ins)
+            data = [where, static, exchange(send)]
         else:
-            moment = call(
-                last_kernel,
-                jax.ShapeDtypeStruct(cotangent.shape, F32),
-                ins,
-                smem_first=True,
-            )
+            moment = call(last_kernel, jax.ShapeDtypeStruct(cotangent.shape, F32), ins)
     return moment
 
 

time: 119 us -> 89.6 us (0.75)
  Pallas kernels: 69.8 us -> 43.2 us
  waiting for transfers between devices: 14.5 us -> 18.1 us
  local copies, waits for them, and re-layouts: 4.15 us -> 0.74 us
  blocking collectives: 13.8 us -> 12.3 us
  other arithmetic: 2.19 us -> 0.81 us
    pallas_call x7, Pallas kernels: 69.8 us -> 43.2 us  [call(): pl.pallas_call(body, out_shape=outs, in_specs=in_vmem(len(ins), smem_firs...]
    all_to_all x3, waiting for transfers between devices: 14.5 us -> 18.1 us  [exchange(): return lax.all_to_all(value, AXES, split_axis=0, concat_axis=0, tiled=True)]
    all_to_all x1, blocking collectives: 13.8 us -> 12.3 us  [exchange(): return lax.all_to_all(value, AXES, split_axis=0, concat_axis=0, tiled=True)]
    broadcast_in_dim x2 -> x0, local copies, waits for them, and re-layouts: 1.35 us -> none  [the longest x1 0.69 us: shards(): phase = jnp.broadcast_to(phase[:, :, None], (8, MODES, lanes))]
    unnamed x6 -> x16, local copies, waits for them, and re-layouts: 1.37 us -> 0.04 us
  transfers between devices with their start and end apart: 3 -> 3, of which waited for: 3 -> 3; matrix products, arithmetic and copies ran while one was open for 2% -> 2% of each run, Pallas kernels for 12% -> 13%
where the time goes in v1:
time: 89.6 us; the launch traced here: 89.2 us
  Pallas kernels  43.2 us (48%)
  waiting for transfers between devices  18.1 us (20%)
  starting transfers between devices  13.9 us (16%)
  blocking collectives  12.3 us (14%)
    pallas_call x7, Pallas kernels, call(): pl.pallas_call(body, out_shape=outs, in_specs=in_vmem(len(ins), smem_firs...  43.2 us
    all_to_all x3, waiting for transfers between devices, exchange(): return lax.all_to_all(value, AXES, split_axis=0, concat_axis=0, tiled=True)  18.1 us
    all_to_all x3, starting transfers between devices, exchange(): return lax.all_to_all(value, AXES, split_axis=0, concat_axis=0, tiled=True)  13.9 us
    all_to_all x1, blocking collectives, exchange(): return lax.all_to_all(value, AXES, split_axis=0, concat_axis=0, tiled=True)  12.3 us
  transfers between devices with their start and end apart: 3, of which 3 were waited for; matrix products, arithmetic and copies ran while one was open for 2% of the time, Pallas kernels for 13%

profile of v1, /device:TPU:0, one launch (start us, length us, event | category | flops | bytes accessed | tf_op | source)
XLA Modules:
  0.0 89.2 jit_solution(17145930824739368879)
XLA Ops:
  0.0 1.8 %shard_map.100 = (f32[32,7,4,128]{3,2,1,0:T(4,128)}, f32[4,128]{1,0:T(4,128)}, f32[3,4,128]{2,1,0:T(4,128)}) custom-call(f32[3,2,2,128]{3,2,1,0:T(2,128)} %cot_ref.5, f32[2,2,128]{2,1,0:T(2,128)} %polar_ref.1, s32[3,2,2,128]{3,2,1,0:T(2,128)} %offset_ref.1, f32[3,2,2,128]{3,2,1,0:T(2,128)} %fraction_ref.1, s32[2,2,16]{2,1,0:T(2,128)} %count_ref.1), custom_call_target="tpu_custom_call" | custom-call | flops 1000 | bytes 100000 | tf_op jit(solution)/shard_map/pallas_call | solution.py:505
  1.8 7.3 %all-to-all-start = ((f32[32,7,4,128]{3,2,1,0:T(4,128)}), f32[32,7,4,128]{3,2,1,0:T(4,128)S(1)}, u32[]{:S(2)}, u32[]{:S(2)}) async-start(f32[32,7,4,128]{3,2,1,0:T(4,128)} %get-tuple-element.12), calls=%async_computation | async-start | bytes 917504 | tf_op jit(solution)/shard_map/all_to_all | solution.py:551
  9.1 0.0 copy-start.3
  9.3 0.1 mul.191
  9.4 0.1 mul.192
  9.5 0.1 mul.186
  9.6 0.1 add.113
  9.6 0.1 add.114
  9.7 0.1 or.13
  9.8 0.1 or.14
  9.9 0.1 and.45
  9.9 0.1 and.46
  10.1 0.1 broadcast_and_fusion
  10.1 0.1 broadcast_add_fusion
  10.2 0.0 copy-start.7
  10.2 0.4 fusion.9.rest_0_.green_ref
  10.6 0.1 pad_add_fusion.where_ref
  10.7 11.5 %all-to-all-done.static_ref.place_ref = f32[32,7,4,128]{3,2,1,0:T(4,128)S(1)} async-done(((f32[32,7,4,128]{3,2,1,0:T(4,128)}), f32[32,7,4,128]{3,2,1,0:T(4,128)S(1)}, u32[]{:S(2)}, u32[]{:S(2)}) %all-to-all-start) | async-done | bytes 458784 | tf_op jit(solution)/shard_map/all_to_all | solution.py:551
  22.2 0.0 copy-done.5
  22.3 14.2 %shard_map.102 = f32[32,3,4,128]{3,2,1,0:T(4,128)} custom-call(s32[3]{0:T(128)S(1)} %pad_add_fusion.where_ref, f32[32,7,4,128]{3,2,1,0:T(4,128)S(1)} %all-to-all-done.static_ref.place_ref, f32[512,128]{1,0:T(8,128)S(1)} %fusion.9.rest_0_.green_ref, bf16[4,128,128]{2,1,0:T(8,128)(2,1)S(1)} %copy-done.5, bf16[4,128,128]{2,1,0:T(8,128)(2,1)S(1)} %copy-done.6, ...), custom_call_target="tpu_custom_call" | custom-call | flops 1000000000 | bytes 100000 | tf_op jit(solution)/shard_map/pallas_call | solution.py:505
  36.4 4.0 %all-to-all-start.1 = ((f32[32,3,4,128]{3,2,1,0:T(4,128)}), f32[32,3,4,128]{3,2,1,0:T(4,128)S(1)}, u32[]{:S(2)}, u32[]{:S(2)}) async-start(f32[32,3,4,128]{3,2,1,0:T(4,128)} %shard_map.102), calls=%async_computation.1 | async-start | bytes 393216 | tf_op jit(solution)/shard_map/all_to_all | solution.py:551
  40.4 0.0 copy-start
  40.4 0.0 copy-start.2
  40.4 6.0 %shard_map.101.near_ref = f32[3,4,128]{2,1,0:T(4,128)S(1)} custom-call(s32[3]{0:T(128)S(1)} %pad_add_fusion.where_ref, f32[32,7,4,128]{3,2,1,0:T(4,128)S(1)} %all-to-all-done.static_ref.place_ref), custom_call_target="tpu_custom_call" | custom-call | flops 100000000 | bytes 100000 | tf_op jit(solution)/shard_map/pallas_call | solution.py:505
  46.5 3.3 %all-to-all-done.1.far_ref = f32[32,3,4,128]{3,2,1,0:T(4,128)S(1)} async-done(((f32[32,3,4,128]{3,2,1,0:T(4,128)}), f32[32,3,4,128]{3,2,1,0:T(4,128)S(1)}, u32[]{:S(2)}, u32[]{:S(2)}) %all-to-all-start.1) | async-done | bytes 196640 | tf_op jit(solution)/shard_map/all_to_all | solution.py:551
  49.7 0.3 shard_map.103
  50.0 12.3 %all_to_all.20.moment_ref = f32[32,3,4,128]{3,2,1,0:T(4,128)S(1)} all-to-all(f32[32,3,4,128]{3,2,1,0:T(4,128)S(1)} %get-tuple-element.14), channel_id=1, replica_groups=mesh['gx'=8,'gy'=4] {'gx','gy'}, dimensions={0} | all-to-all | bytes 393216 | tf_op jit(solution)/shard_map/all_to_all | solution.py:551
  62.4 14.2 %shard_map.105 = f32[32,3,4,128]{3,2,1,0:T(4,128)} custom-call(s32[3]{0:T(128)S(1)} %pad_add_fusion.where_ref, f32[32,7,4,128]{3,2,1,0:T(4,128)S(1)} %all-to-all-done.static_ref.place_ref, f32[32,3,4,128]{3,2,1,0:T(4,128)S(1)} %all_to_all.20.moment_ref, f32[512,128]{1,0:T(8,128)S(1)} %fusion.9.rest_0_.green_ref, bf16[4,128,128]{2,1,0:T(8,128)(2,1)S(1)} %copy-done.5, ...), custom_call_target="tpu_custom_call" | custom-call | flops 1000000000 | bytes 100000 | tf_op jit(solution)/shard_map/pallas_call | solution.py:505
  76.6 2.6 %all-to-all-start.3 = ((f32[32,3,4,128]{3,2,1,0:T(4,128)}), f32[32,3,4,128]{3,2,1,0:T(4,128)S(1)}, u32[]{:S(2)}, u32[]{:S(2)}) async-start(f32[32,3,4,128]{3,2,1,0:T(4,128)} %shard_map.105), calls=%async_computation.3 | async-start | bytes 393216 | tf_op jit(solution)/shard_map/all_to_all | solution.py:551
  79.1 6.0 %shard_map.104.near_ref = f32[3,4,128]{2,1,0:T(4,128)S(1)} custom-call(s32[3]{0:T(128)S(1)} %pad_add_fusion.where_ref, f32[32,7,4,128]{3,2,1,0:T(4,128)S(1)} %all-to-all-done.static_ref.place_ref, f32[32,3,4,128]{3,2,1,0:T(4,128)S(1)} %all_to_all.20.moment_ref), custom_call_target="tpu_custom_call" | custom-call | flops 100000000 | bytes 100000 | tf_op jit(solution)/shard_map/pallas_call | solution.py:505
  85.2 3.3 %all-to-all-done.3.far_ref = f32[32,3,4,128]{3,2,1,0:T(4,128)S(1)} async-done(((f32[32,3,4,128]{3,2,1,0:T(4,128)}), f32[32,3,4,128]{3,2,1,0:T(4,128)S(1)}, u32[]{:S(2)}, u32[]{:S(2)}) %all-to-all-start.3) | async-done | bytes 196640 | tf_op jit(solution)/shard_map/all_to_all | solution.py:551
  88.5 0.7 shard_map.106
  (20 shorter events, 0.2 us)
Async XLA Ops:
  1.8 20.4 %copy-start.4 = (bf16[8,128,128]{2,1,0:T(8,128)(2,1)S(1)}, bf16[8,128,128]{2,1,0:T(8,128)(2,1)}, u32[]{:S(2)}) copy-start(bf16[8,128,128]{2,1,0:T(8,128)(2,1)} %constant.80.clone.rest_4_.ix_low_ref) | copy-start | bytes 786436
  1.8 20.4 %copy-start.6 = (bf16[4,128,128]{2,1,0:T(8,128)(2,1)S(1)}, bf16[4,128,128]{2,1,0:T(8,128)(2,1)}, u32[]{:S(2)}) copy-start(bf16[4,128,128]{2,1,0:T(8,128)(2,1)} %constant.78.clone.rest_2_.fx_low_ref) | copy-start | bytes 393220
  1.8 20.4 %all-to-all-start = ((f32[32,7,4,128]{3,2,1,0:T(4,128)}), f32[32,7,4,128]{3,2,1,0:T(4,128)S(1)}, u32[]{:S(2)}, u32[]{:S(2)}) async-start(f32[32,7,4,128]{3,2,1,0:T(4,128)} %get-tuple-element.12), calls=%async_computation | async-start | bytes 917504 | tf_op jit(solution)/shard_map/all_to_all | solution.py:551
  9.1 13.1 %copy-start.3 = (bf16[8,128,128]{2,1,0:T(8,128)(2,1)S(1)}, bf16[8,128,128]{2,1,0:T(8,128)(2,1)}, u32[]{:S(2)}) copy-start(bf16[8,128,128]{2,1,0:T(8,128)(2,1)} %constant.79.clone.rest_3_.ix_high_ref) | copy-start | bytes 786436
  10.2 12.0 %copy-start.5 = (bf16[4,128,128]{2,1,0:T(8,128)(2,1)S(1)}, bf16[4,128,128]{2,1,0:T(8,128)(2,1)}, u32[]{:S(2)}) copy-start(bf16[4,128,128]{2,1,0:T(8,128)(2,1)} %constant.77.clone.rest_1_.fx_high_ref) | copy-start | bytes 393220
  10.2 12.0 %copy-start.7 = (bf16[64,192]{1,0:T(8,128)(2,1)S(1)}, bf16[64,192]{1,0:T(8,128)(2,1)}, u32[]{:S(2)}) copy-start(bf16[64,192]{1,0:T(8,128)(2,1)} %constant.81.clone.rest_5_.y_ref) | copy-start | bytes 73732
  36.4 13.3 %all-to-all-start.1 = ((f32[32,3,4,128]{3,2,1,0:T(4,128)}), f32[32,3,4,128]{3,2,1,0:T(4,128)S(1)}, u32[]{:S(2)}, u32[]{:S(2)}) async-start(f32[32,3,4,128]{3,2,1,0:T(4,128)} %shard_map.102), calls=%async_computation.1 | async-start | bytes 393216 | tf_op jit(solution)/shard_map/all_to_all | solution.py:551
  40.4 9.3 %copy-start = (f32[3,2,2,128]{3,2,1,0:T(2,128)S(1)}, f32[3,2,2,128]{3,2,1,0:T(2,128)}, u32[]{:S(2)}) copy-start(f32[3,2,2,128]{3,2,1,0:T(2,128)} %cot_ref.5) | copy-start | bytes 18436
  40.4 9.3 %copy-start.2 = (f32[3,4,128]{2,1,0:T(4,128)S(1)}, f32[3,4,128]{2,1,0:T(4,128)}, u32[]{:S(2)}) copy-start(f32[3,4,128]{2,1,0:T(4,128)} %get-tuple-element.11.moment_ref) | copy-start | bytes 18436
  46.5 3.3 %copy-start.1 = (f32[4,128]{1,0:T(4,128)S(1)}, f32[4,128]{1,0:T(4,128)}, u32[]{:S(2)}) copy-start(f32[4,128]{1,0:T(4,128)} %get-tuple-element.10.gain_ref) | copy-start | bytes 6148
  76.6 11.9 %all-to-all-start.3 = ((f32[32,3,4,128]{3,2,1,0:T(4,128)}), f32[32,3,4,128]{3,2,1,0:T(4,128)S(1)}, u32[]{:S(2)}, u32[]{:S(2)}) async-start(f32[32,3,4,128]{3,2,1,0:T(4,128)} %shard_map.105), calls=%async_computation.3 | async-start | bytes 393216 | tf_op jit(solution)/shard_map/all_to_all | solution.py:551

commit v2 on v1

--- a/solution.py
+++ b/solution.py
@@ -20,7 +20,7 @@
 ROOT_PI = 1.7724538509055159
 SELF_GAIN = 4.0 * BETA * BETA * BETA / (3.0 * ROOT_PI)
 MODES = 8
-STATIC_UNROLL = 2
+STATIC_UNROLL = 8
 SPAN = 16
 AXES = ("gx", "gy")
 F32 = jnp.float32
@@ -149,24 +149,24 @@
     ix_low_ref,
     y_ref,
     out_ref,
+    side_ref,
+    form_ref,
     cell_ref,
     line_ref,
     wave_ref,
-    side_ref,
-    rise_ref,
-    edge_ref,
 ):
+    edge = 2 * SPAN
     devices_x, devices_y, cells_x, cells_y, points_z = shape
     columns = cells_x * cells_y
     lanes = place_ref.shape[3]
-    length_x = green_ref.shape[1]
-    length_y = y_ref.shape[0]
-    tall = length_y * MODES
+    length_x = line_ref.shape[0] * line_ref.shape[2]
+    tall = line_ref.shape[1]
+    length_y = tall // MODES
     spill = 3 * MODES
     reach = (HY + 3) * MODES
     per_cell = HY * MODES
     turn_x = 4 // cells_x
-    keep = side_ref.shape[0] > 1
+    keep = form_ref.shape[0] > 1
     unroll = min(4, devices_y)
     layer = (lax.broadcasted_iota(jnp.int32, (1, lanes), 1) // A) * HZ
     mode = where_ref[2] * MODES + lax.broadcasted_iota(jnp.int32, (MODES, lanes), 0)
@@ -175,7 +175,6 @@
         cosine, sine = turns(lax.rem(mode * order, points_z), points_z)
         plus.append(cosine + sine)
         minus.append(cosine - sine)
-    cell_ref[...] = jnp.zeros_like(cell_ref)
 
     def statics(d):
         k = d if keep else 0
@@ -189,10 +188,9 @@
             weights = [[[v[row] for v in kind] for kind in part] for part in parts]
             slopes_x = basis(anchor[0], weights[0][1])
             values_x = basis(anchor[0], weights[0][0])
-            side = jnp.concatenate([slopes_x, values_x], axis=1)
-            high, low = split(side)
+            high, low = split(jnp.concatenate([slopes_x, values_x], axis=1))
             side_ref[k, l] = jnp.concatenate([high, low], axis=0)
-            rise_ref[k, l] = jnp.concatenate(
+            form_ref[k, l, :edge] = jnp.concatenate(
                 [basis(anchor[1], weights[1][0]), basis(anchor[1], weights[1][1])], axis=0
             )
             cosine, sine = turns(lax.rem(mode * (anchor[2] + layer), points_z), points_z)
@@ -204,31 +202,27 @@
                     up = up + kind[order] * plus[order]
                     down = down + kind[order] * minus[order]
                 found.append(cosine * up + sine * down)
-            edge_ref[k, l] = jnp.concatenate(found, axis=0)
-
-    def spread(d, l, slot, group, start):
+            form_ref[k, l, edge:] = jnp.concatenate(found, axis=0)
+
+    def spread_parts(d, l, slot):
         k = d if keep else 0
-        first = edge_ref[k, l, :MODES] * moment_ref[d, lead, l : l + 1, :]
-        second = edge_ref[k, l, :MODES] * moment_ref[d, lead + 1, l : l + 1, :]
-        third = edge_ref[k, l, MODES:] * moment_ref[d, lead + 2, l : l + 1, :]
+        first = form_ref[k, l, edge : edge + MODES] * moment_ref[d, lead, l : l + 1, :]
+        second = form_ref[k, l, edge : edge + MODES] * moment_ref[d, lead + 1, l : l + 1, :]
+        third = form_ref[k, l, edge + MODES :] * moment_ref[d, lead + 2, l : l + 1, :]
         tiles = []
         for y in range(HY + 3):
-            value = rise_ref[k, l, y : y + 1, :]
-            slope = rise_ref[k, l, SPAN + y : SPAN + y + 1, :]
+            value = form_ref[k, l, y : y + 1, :]
+            slope = form_ref[k, l, SPAN + y : SPAN + y + 1, :]
             tile = jnp.concatenate([value * first, slope * second + value * third], axis=1)
             rest = tile - tile.astype(BF16).astype(F32)
             tiles.append(jnp.concatenate([tile, rest], axis=0).astype(BF16))
-        sums = jnp.concatenate(tiles, axis=0)
         pieces = []
         if slot:
             pieces.append(jnp.zeros((slot * 2 * SPAN, 2 * lanes), BF16))
         pieces.append(side_ref[k, l])
         if slot < 3:
             pieces.append(jnp.zeros(((3 - slot) * 2 * SPAN, 2 * lanes), BF16))
-        got = dot_nt(sums, jnp.concatenate(pieces, axis=0))
-        got = got.reshape(HY + 3, 2, MODES, got.shape[1])
-        got = (got[:, 0] + got[:, 1]).reshape(reach, got.shape[3])
-        cell_ref[group, pl.ds(start, reach), :] = cell_ref[group, pl.ds(start, reach), :] + got
+        return jnp.concatenate(tiles, axis=0), jnp.concatenate(pieces, axis=0)
 
     def prepare(d, carry):
         statics(d)
@@ -238,31 +232,37 @@
         lax.fori_loop(0, devices_x * devices_y, prepare, 0, unroll=STATIC_UNROLL)
 
     def spread_row(pair, carry):
-        for odd in range(turn_x):
-            gx = pair * turn_x + odd
-
-            def spread_device(gy, inner):
-                d = gx * devices_y + gy
+        def spread_device(gy, over):
+            parts = [[] for _ in range(cells_y)]
+            for odd in range(turn_x):
+                d = (pair * turn_x + odd) * devices_y + gy
                 if not keep:
                     statics(d)
                 for l in range(columns):
-                    slot = odd * cells_x + l // cells_y
-                    start = pl.multiple_of(
-                        (gy * cells_y + l % cells_y) * per_cell, per_cell
-                    )
-                    spread(d, l, slot, pair, start)
-                return inner
-
-            lax.fori_loop(0, devices_y, spread_device, 0, unroll=unroll)
+                    left, right = spread_parts(d, l, odd * cells_x + l // cells_y)
+                    parts[l % cells_y].append((left, right))
+            for low in range(cells_y):
+                start = pl.multiple_of((gy * cells_y + low) * per_cell, per_cell)
+                left, right = (jnp.concatenate(part, axis=1) for part in zip(*parts[low]))
+                got = dot_nt(left, right).reshape(HY + 3, 2, MODES, 8 * SPAN)
+                got = (got[:, 0] + got[:, 1]).reshape(reach, 8 * SPAN)
+                cell_ref[pair, pl.ds(start, spill), :] = got[:spill] + over
+                cell_ref[pair, pl.ds(start + spill, per_cell - spill), :] = got[spill:per_cell]
+                over = got[per_cell:]
+            return over
+
+        over = lax.fori_loop(
+            0, devices_y, spread_device, jnp.zeros((spill, 8 * SPAN), F32), unroll=unroll
+        )
+        cell_ref[pair, :spill, :] = cell_ref[pair, :spill, :] + over
         return carry
 
     lax.fori_loop(0, devices_x // turn_x, spread_row, 0)
 
-    cell_ref[:, :spill, :] = cell_ref[:, :spill, :] + cell_ref[:, tall : tall + spill, :]
     total = jnp.zeros((tall, length_x), F32)
     for group in range(0, cell_ref.shape[0], 2):
-        one_high, one_low = split(cell_ref[group, :tall, :])
-        two_high, two_low = split(cell_ref[group + 1, :tall, :])
+        one_high, one_low = split(cell_ref[group])
+        two_high, two_low = split(cell_ref[group + 1])
         one, two = fx_high_ref[group], fx_high_ref[group + 1]
         total = total + dot(
             jnp.concatenate([one_high, one_low], axis=1), jnp.concatenate([one, one], axis=0)
@@ -314,23 +314,23 @@
 
     def gather(d, l, slot, group, start):
         k = d if keep else 0
-        high = side_ref[k, l, :SPAN]
-        low = side_ref[k, l, SPAN:]
+        found = side_ref[k, l]
+        high, low = found[:SPAN], found[SPAN:]
         block = [high, high, low, low]
         zero = jnp.zeros((4 * SPAN, 2 * lanes), BF16)
         pieces = [zero] + block if slot else block + [zero]
         got = dot(wave_ref[group, pl.ds(start, window), :], jnp.concatenate(pieces, axis=0))
         sums = [jnp.zeros((MODES, lanes), F32) for _ in range(3)]
         for y in range(HY + 3):
-            value = rise_ref[k, l, y : y + 1, :]
-            slope = rise_ref[k, l, SPAN + y : SPAN + y + 1, :]
+            value = form_ref[k, l, y : y + 1, :]
+            slope = form_ref[k, l, SPAN + y : SPAN + y + 1, :]
             sloped = got[y * MODES : (y + 1) * MODES, :lanes]
             plain = got[y * MODES : (y + 1) * MODES, lanes:]
             sums[0] = sums[0] + sloped * value
             sums[1] = sums[1] + plain * slope
             sums[2] = sums[2] + plain * value
-        value = edge_ref[k, l, :MODES]
-        slope = edge_ref[k, l, MODES:]
+        value = form_ref[k, l, edge : edge + MODES]
+        slope = form_ref[k, l, edge + MODES :]
         return [
             -jnp.sum(sums[axis] * part, axis=0, keepdims=True)
             for axis, part in enumerate((value, value, slope))
@@ -490,23 +490,20 @@
             out_ref[axis, cx] = gain[rows] * (cot_ref[axis, cx] + field[rows])
 
 
-def in_vmem(count, smem_first=False):
-    specs = [pl.BlockSpec(memory_space=pltpu.VMEM)] * count
+def spaces(count, smem_first=False):
+    found = [pl.BlockSpec(memory_space=pltpu.VMEM)] * count
     if smem_first:
-        specs[0] = pl.BlockSpec(memory_space=pltpu.SMEM)
-    return specs
+        found[0] = pl.BlockSpec(memory_space=pltpu.SMEM)
+    return found
 
 
 def call(body, outs, ins, scratch=(), smem_first=False, flops=1000, limit=12):
     many = isinstance(outs, (list, tuple))
-    out_specs = [pl.BlockSpec(memory_space=pltpu.VMEM)] * len(outs) if many else pl.BlockSpec(
-        memory_space=pltpu.VMEM
-    )
     return pl.pallas_call(
         body,
         out_shape=outs,
-        in_specs=in_vmem(len(ins), smem_first),
-        out_specs=out_specs,
+        in_specs=spaces(len(ins), smem_first),
+        out_specs=spaces(len(outs)) if many else spaces(1)[0],
         scratch_shapes=list(scratch),
         compiler_params=pltpu.CompilerParams(vmem_limit_bytes=limit * MIB),
         cost_estimate=pl.CostEstimate(flops=flops, bytes_accessed=100000, transcendentals=0),
@@ -580,40 +577,44 @@
     tall = length_y * MODES
     kept = devices if devices * columns <= 256 else 1
     far_scratch = [
-        pltpu.VMEM((total_x // 4, tall + 3 * MODES, 4 * 2 * SPAN), F32),
+        pltpu.VMEM((total_x // 4, tall, 4 * 2 * SPAN), F32),
         pltpu.VMEM((length_x // 128, tall, 128), F32),
         pltpu.VMEM((total_x // 2, tall + 32, 2 * 4 * SPAN), BF16),
+    ]
+    far_scratch = [
         pltpu.VMEM((kept, columns, 2 * SPAN, 2 * lanes), BF16),
-        pltpu.VMEM((kept, columns, 2 * SPAN, lanes), F32),
-        pltpu.VMEM((kept, columns, 2 * MODES, lanes), F32),
-    ]
+        pltpu.VMEM((kept, columns, 2 * SPAN + 2 * MODES, lanes), F32),
+    ] + far_scratch
     far_shape = (devices_x, devices_y, cells_x, cells_y, length_z)
     near_shape = (devices_x, devices_y, cells_x, cells_y)
 
+    tables = [*(jnp.asarray(t) for t in (*forward, *inverse, y_table))]
+
+
     def far_first(where_ref, static_ref, *rest):
         far_kernel(far_shape, 3, where_ref, static_ref, static_ref, *rest)
 
+    far_later = functools.partial(far_kernel, far_shape, 0)
+
     def near_first(where_ref, static_ref, *rest):
         near_kernel(near_shape, 3, where_ref, static_ref, static_ref, *rest)
 
-    far_later = functools.partial(far_kernel, far_shape, 0)
     near_later = functools.partial(near_kernel, near_shape, 0)
     near_scratch = [
         pltpu.VMEM(((cells_x + 2) * (cells_y + 2) * 7 * A, lanes), F32),
         pltpu.VMEM(((cells_x + 2) * (cells_y + 2), 7, A, lanes), F32),
         pltpu.VMEM((3, A, lanes), F32),
     ]
-    tables = [green, *(jnp.asarray(t) for t in (*forward, *inverse, y_table))]
     data = [where, static]
     for turn in range(ITERS):
         partial = call(
             far_later if turn else far_first,
             moment_shape,
-            data + tables,
+            data + [green] + tables,
             far_scratch,
             smem_first=True,
             flops=10**9,
-            limit=20 if kept > 1 else 58,
+            limit=20 if kept > 1 else 60,
         )
         partial = exchange(partial)
         close = call(

time: 89.6 us -> 89 us (level)
  transfers between devices with their start and end apart: 3 -> 3, of which waited for: 3 -> 3; matrix products, arithmetic and copies ran while one was open for 2% -> 2% of each run, Pallas kernels for 13% -> 14%
where the time goes in v2:
time: 89 us; the launch traced here: 88.6 us
  Pallas kernels  42.6 us (48%)
  waiting for transfers between devices  18.1 us (20%)
  starting transfers between devices  13.8 us (16%)
  blocking collectives  12.3 us (14%)
    pallas_call x7, Pallas kernels, call(): pl.pallas_call(body, out_shape=outs, in_specs=spaces(len(ins), smem_first...  42.6 us
    all_to_all x3, waiting for transfers between devices, exchange(): return lax.all_to_all(value, AXES, split_axis=0, concat_axis=0, tiled=True)  18.1 us
    all_to_all x3, starting transfers between devices, exchange(): return lax.all_to_all(value, AXES, split_axis=0, concat_axis=0, tiled=True)  13.8 us
    all_to_all x1, blocking collectives, exchange(): return lax.all_to_all(value, AXES, split_axis=0, concat_axis=0, tiled=True)  12.3 us
  transfers between devices with their start and end apart: 3, of which 3 were waited for; matrix products, arithmetic and copies ran while one was open for 2% of the time, Pallas kernels for 14%

profile of v2, /device:TPU:0, one launch (start us, length us, event | category | flops | bytes accessed | tf_op | source)
XLA Modules:
  0.0 88.6 jit_solution(4669045790765222215)
XLA Ops:
  0.0 1.8 %shard_map.100 = (f32[32,7,4,128]{3,2,1,0:T(4,128)}, f32[4,128]{1,0:T(4,128)}, f32[3,4,128]{2,1,0:T(4,128)}) custom-call(f32[3,2,2,128]{3,2,1,0:T(2,128)} %cot_ref.5, f32[2,2,128]{2,1,0:T(2,128)} %polar_ref.1, s32[3,2,2,128]{3,2,1,0:T(2,128)} %offset_ref.1, f32[3,2,2,128]{3,2,1,0:T(2,128)} %fraction_ref.1, s32[2,2,16]{2,1,0:T(2,128)} %count_ref.1), custom_call_target="tpu_custom_call" | custom-call | flops 1000 | bytes 100000 | tf_op jit(solution)/shard_map/pallas_call | solution.py:502
  1.8 7.3 %all-to-all-start = ((f32[32,7,4,128]{3,2,1,0:T(4,128)}), f32[32,7,4,128]{3,2,1,0:T(4,128)S(1)}, u32[]{:S(2)}, u32[]{:S(2)}) async-start(f32[32,7,4,128]{3,2,1,0:T(4,128)} %get-tuple-element.12), calls=%async_computation | async-start | bytes 917504 | tf_op jit(solution)/shard_map/all_to_all | solution.py:548
  9.1 0.0 copy-start.3
  9.3 0.1 mul.191
  9.4 0.1 mul.192
  9.5 0.1 mul.186
  9.6 0.1 add.113
  9.6 0.1 add.114
  9.7 0.1 or.13
  9.8 0.1 or.14
  9.9 0.1 and.45
  9.9 0.1 and.46
  10.1 0.1 broadcast_and_fusion
  10.1 0.1 broadcast_add_fusion
  10.2 0.0 copy-start.7
  10.2 0.4 fusion.9.rest_0_.green_ref
  10.6 0.1 pad_add_fusion.where_ref
  10.7 11.5 %all-to-all-done.static_ref.place_ref = f32[32,7,4,128]{3,2,1,0:T(4,128)S(1)} async-done(((f32[32,7,4,128]{3,2,1,0:T(4,128)}), f32[32,7,4,128]{3,2,1,0:T(4,128)S(1)}, u32[]{:S(2)}, u32[]{:S(2)}) %all-to-all-start) | async-done | bytes 458784 | tf_op jit(solution)/shard_map/all_to_all | solution.py:548
  22.2 0.0 copy-done.5
  22.3 13.9 %shard_map.102 = f32[32,3,4,128]{3,2,1,0:T(4,128)} custom-call(s32[3]{0:T(128)S(1)} %pad_add_fusion.where_ref, f32[32,7,4,128]{3,2,1,0:T(4,128)S(1)} %all-to-all-done.static_ref.place_ref, f32[512,128]{1,0:T(8,128)S(1)} %fusion.9.rest_0_.green_ref, bf16[4,128,128]{2,1,0:T(8,128)(2,1)S(1)} %copy-done.5, bf16[4,128,128]{2,1,0:T(8,128)(2,1)S(1)} %copy-done.6, ...), custom_call_target="tpu_custom_call" | custom-call | flops 1000000000 | bytes 100000 | tf_op jit(solution)/shard_map/pallas_call | solution.py:502
  36.1 4.0 %all-to-all-start.1 = ((f32[32,3,4,128]{3,2,1,0:T(4,128)}), f32[32,3,4,128]{3,2,1,0:T(4,128)S(1)}, u32[]{:S(2)}, u32[]{:S(2)}) async-start(f32[32,3,4,128]{3,2,1,0:T(4,128)} %shard_map.102), calls=%async_computation.1 | async-start | bytes 393216 | tf_op jit(solution)/shard_map/all_to_all | solution.py:548
  40.1 0.0 copy-start
  40.1 0.0 copy-start.2
  40.1 6.0 %shard_map.101.near_ref = f32[3,4,128]{2,1,0:T(4,128)S(1)} custom-call(s32[3]{0:T(128)S(1)} %pad_add_fusion.where_ref, f32[32,7,4,128]{3,2,1,0:T(4,128)S(1)} %all-to-all-done.static_ref.place_ref), custom_call_target="tpu_custom_call" | custom-call | flops 100000000 | bytes 100000 | tf_op jit(solution)/shard_map/pallas_call | solution.py:502
  46.2 3.3 %all-to-all-done.1.far_ref = f32[32,3,4,128]{3,2,1,0:T(4,128)S(1)} async-done(((f32[32,3,4,128]{3,2,1,0:T(4,128)}), f32[32,3,4,128]{3,2,1,0:T(4,128)S(1)}, u32[]{:S(2)}, u32[]{:S(2)}) %all-to-all-start.1) | async-done | bytes 196640 | tf_op jit(solution)/shard_map/all_to_all | solution.py:548
  49.4 0.3 shard_map.103
  49.7 12.3 %all_to_all.20.moment_ref = f32[32,3,4,128]{3,2,1,0:T(4,128)S(1)} all-to-all(f32[32,3,4,128]{3,2,1,0:T(4,128)S(1)} %get-tuple-element.14), channel_id=1, replica_groups=mesh['gx'=8,'gy'=4] {'gx','gy'}, dimensions={0} | all-to-all | bytes 393216 | tf_op jit(solution)/shard_map/all_to_all | solution.py:548
  62.1 13.9 %shard_map.105 = f32[32,3,4,128]{3,2,1,0:T(4,128)} custom-call(s32[3]{0:T(128)S(1)} %pad_add_fusion.where_ref, f32[32,7,4,128]{3,2,1,0:T(4,128)S(1)} %all-to-all-done.static_ref.place_ref, f32[32,3,4,128]{3,2,1,0:T(4,128)S(1)} %all_to_all.20.moment_ref, f32[512,128]{1,0:T(8,128)S(1)} %fusion.9.rest_0_.green_ref, bf16[4,128,128]{2,1,0:T(8,128)(2,1)S(1)} %copy-done.5, ...), custom_call_target="tpu_custom_call" | custom-call | flops 1000000000 | bytes 100000 | tf_op jit(solution)/shard_map/pallas_call | solution.py:502
  75.9 2.6 %all-to-all-start.3 = ((f32[32,3,4,128]{3,2,1,0:T(4,128)}), f32[32,3,4,128]{3,2,1,0:T(4,128)S(1)}, u32[]{:S(2)}, u32[]{:S(2)}) async-start(f32[32,3,4,128]{3,2,1,0:T(4,128)} %shard_map.105), calls=%async_computation.3 | async-start | bytes 393216 | tf_op jit(solution)/shard_map/all_to_all | solution.py:548
  78.5 6.0 %shard_map.104.near_ref = f32[3,4,128]{2,1,0:T(4,128)S(1)} custom-call(s32[3]{0:T(128)S(1)} %pad_add_fusion.where_ref, f32[32,7,4,128]{3,2,1,0:T(4,128)S(1)} %all-to-all-done.static_ref.place_ref, f32[32,3,4,128]{3,2,1,0:T(4,128)S(1)} %all_to_all.20.moment_ref), custom_call_target="tpu_custom_call" | custom-call | flops 100000000 | bytes 100000 | tf_op jit(solution)/shard_map/pallas_call | solution.py:502
  84.6 3.3 %all-to-all-done.3.far_ref = f32[32,3,4,128]{3,2,1,0:T(4,128)S(1)} async-done(((f32[32,3,4,128]{3,2,1,0:T(4,128)}), f32[32,3,4,128]{3,2,1,0:T(4,128)S(1)}, u32[]{:S(2)}, u32[]{:S(2)}) %all-to-all-start.3) | async-done | bytes 196640 | tf_op jit(solution)/shard_map/all_to_all | solution.py:548
  87.9 0.7 shard_map.106
  (20 shorter events, 0.2 us)
Async XLA Ops:
  1.8 20.4 %copy-start.4 = (bf16[8,128,128]{2,1,0:T(8,128)(2,1)S(1)}, bf16[8,128,128]{2,1,0:T(8,128)(2,1)}, u32[]{:S(2)}) copy-start(bf16[8,128,128]{2,1,0:T(8,128)(2,1)} %constant.80.clone.rest_4_.ix_low_ref) | copy-start | bytes 786436
  1.8 20.4 %copy-start.6 = (bf16[4,128,128]{2,1,0:T(8,128)(2,1)S(1)}, bf16[4,128,128]{2,1,0:T(8,128)(2,1)}, u32[]{:S(2)}) copy-start(bf16[4,128,128]{2,1,0:T(8,128)(2,1)} %constant.78.clone.rest_2_.fx_low_ref) | copy-start | bytes 393220
  1.8 20.4 %all-to-all-start = ((f32[32,7,4,128]{3,2,1,0:T(4,128)}), f32[32,7,4,128]{3,2,1,0:T(4,128)S(1)}, u32[]{:S(2)}, u32[]{:S(2)}) async-start(f32[32,7,4,128]{3,2,1,0:T(4,128)} %get-tuple-element.12), calls=%async_computation | async-start | bytes 917504 | tf_op jit(solution)/shard_map/all_to_all | solution.py:548
  9.1 13.1 %copy-start.3 = (bf16[8,128,128]{2,1,0:T(8,128)(2,1)S(1)}, bf16[8,128,128]{2,1,0:T(8,128)(2,1)}, u32[]{:S(2)}) copy-start(bf16[8,128,128]{2,1,0:T(8,128)(2,1)} %constant.79.clone.rest_3_.ix_high_ref) | copy-start | bytes 786436
  10.2 12.0 %copy-start.5 = (bf16[4,128,128]{2,1,0:T(8,128)(2,1)S(1)}, bf16[4,128,128]{2,1,0:T(8,128)(2,1)}, u32[]{:S(2)}) copy-start(bf16[4,128,128]{2,1,0:T(8,128)(2,1)} %constant.77.clone.rest_1_.fx_high_ref) | copy-start | bytes 393220
  10.2 12.0 %copy-start.7 = (bf16[64,192]{1,0:T(8,128)(2,1)S(1)}, bf16[64,192]{1,0:T(8,128)(2,1)}, u32[]{:S(2)}) copy-start(bf16[64,192]{1,0:T(8,128)(2,1)} %constant.81.clone.rest_5_.y_ref) | copy-start | bytes 73732
  36.1 13.3 %all-to-all-start.1 = ((f32[32,3,4,128]{3,2,1,0:T(4,128)}), f32[32,3,4,128]{3,2,1,0:T(4,128)S(1)}, u32[]{:S(2)}, u32[]{:S(2)}) async-start(f32[32,3,4,128]{3,2,1,0:T(4,128)} %shard_map.102), calls=%async_computation.1 | async-start | bytes 393216 | tf_op jit(solution)/shard_map/all_to_all | solution.py:548
  40.1 9.3 %copy-start = (f32[3,2,2,128]{3,2,1,0:T(2,128)S(1)}, f32[3,2,2,128]{3,2,1,0:T(2,128)}, u32[]{:S(2)}) copy-start(f32[3,2,2,128]{3,2,1,0:T(2,128)} %cot_ref.5) | copy-start | bytes 18436
  40.1 9.3 %copy-start.2 = (f32[3,4,128]{2,1,0:T(4,128)S(1)}, f32[3,4,128]{2,1,0:T(4,128)}, u32[]{:S(2)}) copy-start(f32[3,4,128]{2,1,0:T(4,128)} %get-tuple-element.11.moment_ref) | copy-start | bytes 18436
  46.1 3.3 %copy-start.1 = (f32[4,128]{1,0:T(4,128)S(1)}, f32[4,128]{1,0:T(4,128)}, u32[]{:S(2)}) copy-start(f32[4,128]{1,0:T(4,128)} %get-tuple-element.10.gain_ref) | copy-start | bytes 6148
  75.9 11.9 %all-to-all-start.3 = ((f32[32,3,4,128]{3,2,1,0:T(4,128)}), f32[32,3,4,128]{3,2,1,0:T(4,128)S(1)}, u32[]{:S(2)}, u32[]{:S(2)}) async-start(f32[32,3,4,128]{3,2,1,0:T(4,128)} %shard_map.105), calls=%async_computation.3 | async-start | bytes 393216 | tf_op jit(solution)/shard_map/all_to_all | solution.py:548

commit v3 on v2

--- a/solution.py
+++ b/solution.py
@@ -20,6 +20,7 @@
 ROOT_PI = 1.7724538509055159
 SELF_GAIN = 4.0 * BETA * BETA * BETA / (3.0 * ROOT_PI)
 MODES = 8
+SIXTH = 1.0 / 6.0
 STATIC_UNROLL = 8
 SPAN = 16
 AXES = ("gx", "gy")
@@ -69,10 +70,10 @@
     square = fraction * fraction
     cube = square * fraction
     values = (
-        rest * rest * rest / 6.0,
-        (3.0 * cube - 6.0 * square + 4.0) / 6.0,
-        (-3.0 * cube + 3.0 * square + 3.0 * fraction + 1.0) / 6.0,
-        cube / 6.0,
+        rest * rest * rest * SIXTH,
+        (3.0 * cube - 6.0 * square + 4.0) * SIXTH,
+        (-3.0 * cube + 3.0 * square + 3.0 * fraction + 1.0) * SIXTH,
+        cube * SIXTH,
     )
     slopes = (
         -0.5 * rest * rest,
@@ -90,6 +91,12 @@
     for order in range(4):
         total = jnp.where(index == order, weights[order], total)
     return total
+
+
+def around(count, length):
+    if length & (length - 1):
+        return lax.rem(count, length)
+    return count & (length - 1)
 
 
 def turns(count, length):
@@ -193,7 +200,7 @@
             form_ref[k, l, :edge] = jnp.concatenate(
                 [basis(anchor[1], weights[1][0]), basis(anchor[1], weights[1][1])], axis=0
             )
-            cosine, sine = turns(lax.rem(mode * (anchor[2] + layer), points_z), points_z)
+            cosine, sine = turns(around(mode * (anchor[2] + layer), points_z), points_z)
             found = []
             for kind in weights[2]:
                 up = kind[0] * plus[0]

time: 89 us -> 88.9 us (level)
  no operation moved by 1% of the time
where the time goes in v3:
time: 88.9 us; the launch traced here: 88.5 us
  Pallas kernels  42.5 us (48%)
  waiting for transfers between devices  18.1 us (20%)
  starting transfers between devices  13.8 us (16%)
  blocking collectives  12.3 us (14%)
    pallas_call x7, Pallas kernels, call(): pl.pallas_call(body, out_shape=outs, in_specs=spaces(len(ins), smem_first...  42.5 us
    all_to_all x3, waiting for transfers between devices, exchange(): return lax.all_to_all(value, AXES, split_axis=0, concat_axis=0, tiled=True)  18.1 us
    all_to_all x3, starting transfers between devices, exchange(): return lax.all_to_all(value, AXES, split_axis=0, concat_axis=0, tiled=True)  13.8 us
    all_to_all x1, blocking collectives, exchange(): return lax.all_to_all(value, AXES, split_axis=0, concat_axis=0, tiled=True)  12.3 us
  transfers between devices with their start and end apart: 3, of which 3 were waited for; matrix products, arithmetic and copies ran while one was open for 2% of the time, Pallas kernels for 14%

profile of v3, /device:TPU:0, one launch (start us, length us, event | category | flops | bytes accessed | tf_op | source)
XLA Modules:
  0.0 88.5 jit_solution(10371093886657920022)
XLA Ops:
  0.0 1.8 %shard_map.100 = (f32[32,7,4,128]{3,2,1,0:T(4,128)}, f32[4,128]{1,0:T(4,128)}, f32[3,4,128]{2,1,0:T(4,128)}) custom-call(f32[3,2,2,128]{3,2,1,0:T(2,128)} %cot_ref.5, f32[2,2,128]{2,1,0:T(2,128)} %polar_ref.1, s32[3,2,2,128]{3,2,1,0:T(2,128)} %offset_ref.1, f32[3,2,2,128]{3,2,1,0:T(2,128)} %fraction_ref.1, s32[2,2,16]{2,1,0:T(2,128)} %count_ref.1), custom_call_target="tpu_custom_call" | custom-call | flops 1000 | bytes 100000 | tf_op jit(solution)/shard_map/pallas_call | solution.py:509
  1.8 7.3 %all-to-all-start = ((f32[32,7,4,128]{3,2,1,0:T(4,128)}), f32[32,7,4,128]{3,2,1,0:T(4,128)S(1)}, u32[]{:S(2)}, u32[]{:S(2)}) async-start(f32[32,7,4,128]{3,2,1,0:T(4,128)} %get-tuple-element.12), calls=%async_computation | async-start | bytes 917504 | tf_op jit(solution)/shard_map/all_to_all | solution.py:555
  9.1 0.0 copy-start.3
  9.3 0.1 mul.191
  9.4 0.1 mul.192
  9.5 0.1 mul.186
  9.6 0.1 add.113
  9.6 0.1 add.114
  9.7 0.1 or.13
  9.8 0.1 or.14
  9.9 0.1 and.45
  9.9 0.1 and.46
  10.1 0.1 broadcast_and_fusion
  10.1 0.1 broadcast_add_fusion
  10.2 0.0 copy-start.7
  10.2 0.4 fusion.9.rest_0_.green_ref
  10.6 0.1 pad_add_fusion.where_ref
  10.7 11.5 %all-to-all-done.static_ref.place_ref = f32[32,7,4,128]{3,2,1,0:T(4,128)S(1)} async-done(((f32[32,7,4,128]{3,2,1,0:T(4,128)}), f32[32,7,4,128]{3,2,1,0:T(4,128)S(1)}, u32[]{:S(2)}, u32[]{:S(2)}) %all-to-all-start) | async-done | bytes 458784 | tf_op jit(solution)/shard_map/all_to_all | solution.py:555
  22.2 0.0 copy-done.5
  22.3 13.8 %shard_map.102 = f32[32,3,4,128]{3,2,1,0:T(4,128)} custom-call(s32[3]{0:T(128)S(1)} %pad_add_fusion.where_ref, f32[32,7,4,128]{3,2,1,0:T(4,128)S(1)} %all-to-all-done.static_ref.place_ref, f32[512,128]{1,0:T(8,128)S(1)} %fusion.9.rest_0_.green_ref, bf16[4,128,128]{2,1,0:T(8,128)(2,1)S(1)} %copy-done.5, bf16[4,128,128]{2,1,0:T(8,128)(2,1)S(1)} %copy-done.6, ...), custom_call_target="tpu_custom_call" | custom-call | flops 1000000000 | bytes 100000 | tf_op jit(solution)/shard_map/pallas_call | solution.py:509
  36.1 4.0 %all-to-all-start.1 = ((f32[32,3,4,128]{3,2,1,0:T(4,128)}), f32[32,3,4,128]{3,2,1,0:T(4,128)S(1)}, u32[]{:S(2)}, u32[]{:S(2)}) async-start(f32[32,3,4,128]{3,2,1,0:T(4,128)} %shard_map.102), calls=%async_computation.1 | async-start | bytes 393216 | tf_op jit(solution)/shard_map/all_to_all | solution.py:555
  40.0 0.0 copy-start
  40.0 0.0 copy-start.2
  40.1 6.0 %shard_map.101.near_ref = f32[3,4,128]{2,1,0:T(4,128)S(1)} custom-call(s32[3]{0:T(128)S(1)} %pad_add_fusion.where_ref, f32[32,7,4,128]{3,2,1,0:T(4,128)S(1)} %all-to-all-done.static_ref.place_ref), custom_call_target="tpu_custom_call" | custom-call | flops 100000000 | bytes 100000 | tf_op jit(solution)/shard_map/pallas_call | solution.py:509
  46.1 3.3 %all-to-all-done.1.far_ref = f32[32,3,4,128]{3,2,1,0:T(4,128)S(1)} async-done(((f32[32,3,4,128]{3,2,1,0:T(4,128)}), f32[32,3,4,128]{3,2,1,0:T(4,128)S(1)}, u32[]{:S(2)}, u32[]{:S(2)}) %all-to-all-start.1) | async-done | bytes 196640 | tf_op jit(solution)/shard_map/all_to_all | solution.py:555
  49.4 0.3 shard_map.103
  49.7 12.3 %all_to_all.20.moment_ref = f32[32,3,4,128]{3,2,1,0:T(4,128)S(1)} all-to-all(f32[32,3,4,128]{3,2,1,0:T(4,128)S(1)} %get-tuple-element.14), channel_id=1, replica_groups=mesh['gx'=8,'gy'=4] {'gx','gy'}, dimensions={0} | all-to-all | bytes 393216 | tf_op jit(solution)/shard_map/all_to_all | solution.py:555
  62.0 13.8 %shard_map.105 = f32[32,3,4,128]{3,2,1,0:T(4,128)} custom-call(s32[3]{0:T(128)S(1)} %pad_add_fusion.where_ref, f32[32,7,4,128]{3,2,1,0:T(4,128)S(1)} %all-to-all-done.static_ref.place_ref, f32[32,3,4,128]{3,2,1,0:T(4,128)S(1)} %all_to_all.20.moment_ref, f32[512,128]{1,0:T(8,128)S(1)} %fusion.9.rest_0_.green_ref, bf16[4,128,128]{2,1,0:T(8,128)(2,1)S(1)} %copy-done.5, ...), custom_call_target="tpu_custom_call" | custom-call | flops 1000000000 | bytes 100000 | tf_op jit(solution)/shard_map/pallas_call | solution.py:509
  75.8 2.6 %all-to-all-start.3 = ((f32[32,3,4,128]{3,2,1,0:T(4,128)}), f32[32,3,4,128]{3,2,1,0:T(4,128)S(1)}, u32[]{:S(2)}, u32[]{:S(2)}) async-start(f32[32,3,4,128]{3,2,1,0:T(4,128)} %shard_map.105), calls=%async_computation.3 | async-start | bytes 393216 | tf_op jit(solution)/shard_map/all_to_all | solution.py:555
  78.4 6.0 %shard_map.104.near_ref = f32[3,4,128]{2,1,0:T(4,128)S(1)} custom-call(s32[3]{0:T(128)S(1)} %pad_add_fusion.where_ref, f32[32,7,4,128]{3,2,1,0:T(4,128)S(1)} %all-to-all-done.static_ref.place_ref, f32[32,3,4,128]{3,2,1,0:T(4,128)S(1)} %all_to_all.20.moment_ref), custom_call_target="tpu_custom_call" | custom-call | flops 100000000 | bytes 100000 | tf_op jit(solution)/shard_map/pallas_call | solution.py:509
  84.4 3.3 %all-to-all-done.3.far_ref = f32[32,3,4,128]{3,2,1,0:T(4,128)S(1)} async-done(((f32[32,3,4,128]{3,2,1,0:T(4,128)}), f32[32,3,4,128]{3,2,1,0:T(4,128)S(1)}, u32[]{:S(2)}, u32[]{:S(2)}) %all-to-all-start.3) | async-done | bytes 196640 | tf_op jit(solution)/shard_map/all_to_all | solution.py:555
  87.7 0.7 shard_map.106
  (20 shorter events, 0.2 us)
Async XLA Ops:
  1.8 20.4 %copy-start.4 = (bf16[8,128,128]{2,1,0:T(8,128)(2,1)S(1)}, bf16[8,128,128]{2,1,0:T(8,128)(2,1)}, u32[]{:S(2)}) copy-start(bf16[8,128,128]{2,1,0:T(8,128)(2,1)} %constant.80.clone.rest_4_.ix_low_ref) | copy-start | bytes 786436
  1.8 20.4 %copy-start.6 = (bf16[4,128,128]{2,1,0:T(8,128)(2,1)S(1)}, bf16[4,128,128]{2,1,0:T(8,128)(2,1)}, u32[]{:S(2)}) copy-start(bf16[4,128,128]{2,1,0:T(8,128)(2,1)} %constant.78.clone.rest_2_.fx_low_ref) | copy-start | bytes 393220
  1.8 20.4 %all-to-all-start = ((f32[32,7,4,128]{3,2,1,0:T(4,128)}), f32[32,7,4,128]{3,2,1,0:T(4,128)S(1)}, u32[]{:S(2)}, u32[]{:S(2)}) async-start(f32[32,7,4,128]{3,2,1,0:T(4,128)} %get-tuple-element.12), calls=%async_computation | async-start | bytes 917504 | tf_op jit(solution)/shard_map/all_to_all | solution.py:555
  9.1 13.1 %copy-start.3 = (bf16[8,128,128]{2,1,0:T(8,128)(2,1)S(1)}, bf16[8,128,128]{2,1,0:T(8,128)(2,1)}, u32[]{:S(2)}) copy-start(bf16[8,128,128]{2,1,0:T(8,128)(2,1)} %constant.79.clone.rest_3_.ix_high_ref) | copy-start | bytes 786436
  10.2 12.0 %copy-start.5 = (bf16[4,128,128]{2,1,0:T(8,128)(2,1)S(1)}, bf16[4,128,128]{2,1,0:T(8,128)(2,1)}, u32[]{:S(2)}) copy-start(bf16[4,128,128]{2,1,0:T(8,128)(2,1)} %constant.77.clone.rest_1_.fx_high_ref) | copy-start | bytes 393220
  10.2 12.0 %copy-start.7 = (bf16[64,192]{1,0:T(8,128)(2,1)S(1)}, bf16[64,192]{1,0:T(8,128)(2,1)}, u32[]{:S(2)}) copy-start(bf16[64,192]{1,0:T(8,128)(2,1)} %constant.81.clone.rest_5_.y_ref) | copy-start | bytes 73732
  36.1 13.3 %all-to-all-start.1 = ((f32[32,3,4,128]{3,2,1,0:T(4,128)}), f32[32,3,4,128]{3,2,1,0:T(4,128)S(1)}, u32[]{:S(2)}, u32[]{:S(2)}) async-start(f32[32,3,4,128]{3,2,1,0:T(4,128)} %shard_map.102), calls=%async_computation.1 | async-start | bytes 393216 | tf_op jit(solution)/shard_map/all_to_all | solution.py:555
  40.0 9.3 %copy-start = (f32[3,2,2,128]{3,2,1,0:T(2,128)S(1)}, f32[3,2,2,128]{3,2,1,0:T(2,128)}, u32[]{:S(2)}) copy-start(f32[3,2,2,128]{3,2,1,0:T(2,128)} %cot_ref.5) | copy-start | bytes 18436
  40.0 9.3 %copy-start.2 = (f32[3,4,128]{2,1,0:T(4,128)S(1)}, f32[3,4,128]{2,1,0:T(4,128)}, u32[]{:S(2)}) copy-start(f32[3,4,128]{2,1,0:T(4,128)} %get-tuple-element.11.moment_ref) | copy-start | bytes 18436
  46.1 3.3 %copy-start.1 = (f32[4,128]{1,0:T(4,128)S(1)}, f32[4,128]{1,0:T(4,128)}, u32[]{:S(2)}) copy-start(f32[4,128]{1,0:T(4,128)} %get-tuple-element.10.gain_ref) | copy-start | bytes 6148
  75.8 11.9 %all-to-all-start.3 = ((f32[32,3,4,128]{3,2,1,0:T(4,128)}), f32[32,3,4,128]{3,2,1,0:T(4,128)S(1)}, u32[]{:S(2)}, u32[]{:S(2)}) async-start(f32[32,3,4,128]{3,2,1,0:T(4,128)} %shard_map.105), calls=%async_computation.3 | async-start | bytes 393216 | tf_op jit(solution)/shard_map/all_to_all | solution.py:555
